TPU v7x, 32 devices: a whole 2x2x4 slice. The times are simulated.
32 devices in a mesh: expert: 8 (over y, x, core), dp: 4 (over z).
Axes of the slice: x: 2, y: 2, z: 4, core: 2. Of those that a mesh axis runs over, the one named last changes fastest.
Arguments:
- heatmap: bfloat16 [4, 64, 56, 256], P('dp', 'expert'), may hold values from -6 to 6
- labels: int32 [4, 56], P('dp', 'expert'), may hold values from 0 to 7, as said below
- w_in: bfloat16 [8, 2304, 1024], P('expert'), may hold values from -0.125 to 0.125
- w_out: bfloat16 [8, 1024, 256], P('expert'), may hold values from -0.1875 to 0.1875
- b_in: float32 [8, 1024], P('expert'), may hold values from -3 to 3
- cotangent: bfloat16 [4, 64, 56, 256], P('dp', 'expert'), may hold values from -0.29882812 to 0.29882812
Outputs:
- output: bfloat16 [4, 64, 56, 256], P('dp', 'expert')
- grad_w_in: float32 [8, 2304, 1024], P('expert', None, 'dp')
- grad_w_out: float32 [8, 1024, 256], P('expert', 'dp')
- grad_b_in: float32 [8, 1024], P('expert', 'dp')
Inputs may be any that keep to these rules, and one draw needn't show every extreme that they name: `labels`: of the tiles of one image, at most 10 carry one label, and some label of the draw is carried by exactly 10; of the 7 tiles of one tile row, at most 2 carry one label, a bound that is reached.
All inputs are finite; a program needn't handle non-finite values.
Results may differ from a plain program's by a relative error of at most 0.0055.
Values may be sent and summed in bfloat16 or wider, within the bound.
A program may use at most 128 MiB of HBM per device.

v0:
```python
import jax
import jax.numpy as jnp
from jax import lax
from jax.sharding import PartitionSpec as P

CAP = 2


def extended(cells, sides, width):
    for axis, dim in sides:
        count = lax.axis_size(axis)
        ends = count - 1
        head = lax.slice_in_dim(cells, 0, width, axis=dim)
        tail = lax.slice_in_dim(cells, cells.shape[dim] - width, cells.shape[dim], axis=dim)
        cells = jnp.concatenate(
            [
                lax.ppermute(tail, axis, [(i, (i + 1) % count) for i in range(ends)]),
                cells,
                lax.ppermute(head, axis, [((i + 1) % count, i) for i in range(ends)]),
            ],
            axis=dim,
        )
    return cells


def gelu_parts(preact):
    normal_cdf = 0.5 * (1.0 + lax.erf(preact * 0.7071067811865476))
    density = jnp.exp(-0.5 * preact * preact) * 0.3989422804014327
    return (preact * normal_cdf, normal_cdf + preact * density)


def unfold(framed):
    count_tiles = framed.shape[0]
    channels = framed.shape[3]
    windows = []
    for row_shift in range(3):
        for col_shift in range(3):
            windows.append(framed[:, row_shift : row_shift + 8, col_shift : col_shift + 8, :])
    joined = jnp.concatenate(windows, axis=3)
    return joined.reshape(count_tiles * 64, 9 * channels)


def contract_rows(left_side, right_side):
    return lax.dot_general(
        left_side, right_side, (((0,), (0,)), ((), ())), preferred_element_type=jnp.float32
    )


def shards(heatmap, labels, w_in, w_out, b_in, cotangent):
    channels = heatmap.shape[3]
    columns = heatmap.shape[2]
    tile_count = columns // 8
    owners = lax.axis_size("expert")
    slot_total = owners * CAP
    capacity = 3 * tile_count // 2
    bordered = extended(heatmap[0], (("expert", 0),), 1)
    bordered = jnp.pad(bordered, ((0, 0), (1, 7), (0, 0)))
    left_part = bordered[:, :columns].reshape(10, tile_count, 8, channels)
    right_part = bordered[:, 8 : columns + 8].reshape(10, tile_count, 8, channels)[:, :, :2]
    framed = (
        jnp.concatenate([left_part, right_part], axis=2)
        .transpose(1, 0, 2, 3)
        .reshape(tile_count, 100 * channels)
    )
    labels_here = labels[0]
    tile_ids = jnp.arange(tile_count, dtype=jnp.int32)
    earlier = (labels_here[None, :] == labels_here[:, None]) & (
        tile_ids[None, :] < tile_ids[:, None]
    )
    order_rank = jnp.sum(earlier.astype(jnp.int32), axis=1)
    slot_index = labels_here * CAP + order_rank
    send_map = (slot_index[None, :] == jnp.arange(slot_total, dtype=jnp.int32)[:, None]).astype(
        jnp.bfloat16
    )
    occupied = jnp.sum(send_map, axis=1).reshape(owners, CAP)
    outgoing = (
        jnp.dot(send_map, framed, preferred_element_type=jnp.float32)
        .astype(jnp.bfloat16)
        .reshape(owners, CAP, 100 * channels)
    )
    target_tiles = (
        cotangent[0]
        .reshape(8, tile_count, 8, channels)
        .transpose(1, 0, 2, 3)
        .reshape(tile_count, 64 * channels)
    )
    target_out = (
        jnp.dot(send_map, target_tiles, preferred_element_type=jnp.float32)
        .astype(jnp.bfloat16)
        .reshape(owners, CAP, 64 * channels)
    )
    arrived, occupied_in = (
        lax.all_to_all(outgoing, "expert", split_axis=0, concat_axis=0, tiled=True),
        lax.all_to_all(occupied, "expert", split_axis=0, concat_axis=0, tiled=True),
    )
    live_slots = occupied_in.reshape(slot_total).astype(jnp.float32)
    position = jnp.cumsum(live_slots) - live_slots
    take_map = (
        (position[None, :] == jnp.arange(capacity, dtype=jnp.float32)[:, None])
        & (live_slots[None, :] > 0.5)
    ).astype(jnp.bfloat16)
    compact = jnp.dot(
        take_map, arrived.reshape(slot_total, 100 * channels), preferred_element_type=jnp.float32
    ).astype(jnp.bfloat16)
    compact = compact.reshape(capacity, 10, 10, channels)
    patches = unfold(compact)
    preact = jnp.dot(patches, w_in[0], preferred_element_type=jnp.float32) + b_in[0]
    activation, gelu_slope = gelu_parts(preact)
    hidden = activation.astype(jnp.bfloat16)
    result = (
        jnp.dot(hidden, w_out[0], preferred_element_type=jnp.float32)
        .astype(jnp.bfloat16)
        .reshape(capacity, 64 * channels)
    )
    result_slots = (
        contract_rows(take_map, result).astype(jnp.bfloat16).reshape(owners, CAP, 64 * channels)
    )
    returned = lax.all_to_all(result_slots, "expert", split_axis=0, concat_axis=0, tiled=True)
    mine = contract_rows(send_map, returned.reshape(slot_total, 64 * channels)).astype(jnp.bfloat16)
    output = (
        mine.reshape(tile_count, 8, 8, channels)
        .transpose(1, 0, 2, 3)
        .reshape(1, 8, columns, channels)
    )
    target_in = lax.all_to_all(target_out, "expert", split_axis=0, concat_axis=0, tiled=True)
    target_rows = jnp.dot(
        take_map, target_in.reshape(slot_total, 64 * channels), preferred_element_type=jnp.float32
    ).astype(jnp.bfloat16)
    target_rows = target_rows.reshape(capacity * 64, channels)
    grad_second = contract_rows(hidden, target_rows)
    back_hidden = lax.dot_general(
        target_rows, w_out[0], (((1,), (1,)), ((), ())), preferred_element_type=jnp.float32
    )
    hidden_grad = (back_hidden * gelu_slope).astype(jnp.bfloat16)
    grad_bias = jnp.sum(hidden_grad, axis=0, dtype=jnp.float32)
    grad_first = contract_rows(patches, hidden_grad)
    grad_first, grad_second, grad_bias = (
        lax.psum_scatter(grad_first, "dp", scatter_dimension=1, tiled=True),
        lax.psum_scatter(grad_second, "dp", scatter_dimension=0, tiled=True),
        lax.psum_scatter(grad_bias, "dp", scatter_dimension=0, tiled=True),
    )
    return (output, grad_first[None], grad_second[None], grad_bias[None])


def solution(mesh):
    return jax.shard_map(
        shards,
        mesh=mesh,
        in_specs=(
            P("dp", "expert", None, None),
            P("dp", "expert"),
            P("expert", None, None),
            P("expert", None, None),
            P("expert", None),
            P("dp", "expert", None, None),
        ),
        out_specs=(
            P("dp", "expert", None, None),
            P("expert", None, "dp"),
            P("expert", "dp", None),
            P("expert", "dp"),
        ),
        check_vma=False,
    )
```

profile of v0, /device:TPU:1, one launch (start us, length us, event | category | flops | bytes accessed | tf_op | source)
XLA Modules:
  0.0 261.9 jit_solution(11212996133292334027)
XLA Ops:
  7.2 0.9 convert_reduce_fusion.1
  8.1 0.7 fusion.32
  8.9 0.7 all_to_all.20
  9.6 5.2 %all-to-all-start = ((bf16[8,1,2]{2,1,0:T(2,128)(2,1)}), bf16[8,1,2]{2,1,0:T(2,128)(2,1)S(1)}, u32[]{:S(2)}, u32[]{:S(2)}) async-start(bf16[8,1,2]{2,1,0:T(2,128)(2,1)} %all_to_all.20), calls=%async_computation | async-start | bytes 8192 | tf_op jit(solution)/shard_map/all_to_all | solution.py:94
  14.8 0.8 slice_bitcast_fusion.3
  15.6 3.5 %collective-permute-start = (bf16[1,56,256]{2,1,0:T(8,128)(2,1)S(1)}, bf16[1,56,256]{2,1,0:T(8,128)(2,1)S(1)}, u32[]{:S(2)}, u32[]{:S(2)}) collective-permute-start(bf16[1,56,256]{2,1,0:T(8,128)(2,1)S(1)} %get-tuple-element.6), channel_id=1, source_target_pairs={{0,4},{4,8},{8,12},{12,16},{16,20},{20,24},{24,28},{1,5},{5,9},{9,... | collective-permute-start | bytes 86024 | tf_op jit(solution)/shard_map/ppermute | solution.py:17
  19.1 1.9 collective-permute-start.1
  21.0 1.0 copy_bitcast_fusion
  22.6 1.1 reshape.129
  24.4 3.8 %all-to-all-start.3 = ((bf16[8,2,16384]{2,1,0:T(2,128)(2,1)}), bf16[8,2,16384]{2,1,0:T(2,128)(2,1)S(1)}, u32[]{:S(2)}, u32[]{:S(2)}) async-start(bf16[8,2,16384]{2,1,0:T(2,128)(2,1)} %reshape.129), calls=%async_computation.3 | async-start | bytes 1048576 | tf_op jit(solution)/shard_map/all_to_all | solution.py:125
  29.0 1.2 reshape.119
  30.2 4.7 %all-to-all-done.3 = bf16[8,2,16384]{2,1,0:T(2,128)(2,1)S(1)} async-done(((bf16[8,2,16384]{2,1,0:T(2,128)(2,1)}), bf16[8,2,16384]{2,1,0:T(2,128)(2,1)S(1)}, u32[]{:S(2)}, u32[]{:S(2)}) %all-to-all-start.3) | async-done | bytes 524320 | tf_op jit(solution)/shard_map/all_to_all | solution.py:125
  34.9 6.5 %all-to-all-start.1 = ((bf16[8,2,25600]{2,1,0:T(2,128)(2,1)}), bf16[8,2,25600]{2,1,0:T(2,128)(2,1)S(1)}, u32[]{:S(2)}, u32[]{:S(2)}) async-start(bf16[8,2,25600]{2,1,0:T(2,128)(2,1)} %reshape.119), calls=%async_computation.1 | async-start | bytes 1638400 | tf_op jit(solution)/shard_map/all_to_all | solution.py:93
  42.4 8.4 %all-to-all-done.1 = bf16[8,2,25600]{2,1,0:T(2,128)(2,1)S(1)} async-done(((bf16[8,2,25600]{2,1,0:T(2,128)(2,1)}), bf16[8,2,25600]{2,1,0:T(2,128)(2,1)S(1)}, u32[]{:S(2)}, u32[]{:S(2)}) %all-to-all-start.1) | async-done | bytes 819232 | tf_op jit(solution)/shard_map/all_to_all | solution.py:93
  52.7 8.4 %multiply_convert_fusion = (bf16[640,1024]{1,0:T(8,128)(2,1)S(1)}, f32[640,1024]{1,0:T(8,128)}) fusion(f32[1024]{0:T(1024)S(1)} %bitcast.79, bf16[640,2304]{1,0:T(8,128)(2,1)S(1)} %bitcast.73, bf16[1,2304,1024]{2,1,0:T(8,128)(2,1)} %param.8), kind=kOutput, calls=%fused_computation.16 | convolution fusion | flops 3023831040 | bytes 11603968 | tf_op jit(solution)/shard_map/dot_general | solution.py:107
  61.1 1.6 fusion.34
  62.8 3.0 %convert_reduce_fusion = (f32[1024]{0:T(1024)S(1)}, bf16[640,1024]{1,0:T(8,128)(2,1)S(1)}) fusion(f32[640,1024]{1,0:T(8,128)} %get-tuple-element.9, f32[1024]{0:T(1024)S(1)} %bitcast.80, bf16[640,256]{1,0:T(8,128)(2,1)S(1)} %reshape.131, bf16[1,1024,256]{2,1,0:T(8,128)(2,1)S(1)} %copy-done), kind=kOutput, calls=%fused_computation.15 | convolution fusion | flops 344062976 | bytes 4792320 | tf_op jit(solution)/shard_map/dot_general | solution.py:131
  65.8 6.3 %fusion.33 = f32[2304,1024]{1,0:T(8,128)} fusion(bf16[640,2304]{1,0:T(8,128)(2,1)S(1)} %bitcast.74, bf16[640,1024]{1,0:T(8,128)(2,1)S(1)} %get-tuple-element.11), kind=kOutput, calls=%fused_computation.67 | convolution fusion | flops 3019898880 | bytes 13697024 | tf_op jit(solution)/shard_map/dot_general | solution.py:44
  73.3 1.2 reshape.124
  74.4 6.9 %all-to-all-start.2 = ((bf16[8,2,16384]{2,1,0:T(2,128)(2,1)}), bf16[8,2,16384]{2,1,0:T(2,128)(2,1)S(1)}, u32[]{:S(2)}, u32[]{:S(2)}) async-start(bf16[8,2,16384]{2,1,0:T(2,128)(2,1)} %reshape.124), calls=%async_computation.2 | async-start | bytes 1048576 | tf_op jit(solution)/shard_map/all_to_all | solution.py:118
  82.6 10.4 %all-reduce.1 = f32[1024]{0:T(1024)S(1)} all-reduce(f32[1024]{0:T(1024)S(1)} %get-tuple-element.10), channel_id=4, replica_groups=mesh['expert'=8,'dp'=4] {'dp'}, use_global_device_ids=true, to_apply=%region_6.7.clone | all-reduce | flops 1024 | bytes 8192
  93.0 0.6 dynamic-slice.1
  94.1 0.7 copy_bitcast_fusion.1
  94.8 160.2 %reduce-scatter.3.cloned.1.call-done = f32[2304,256]{1,0:T(8,128)} async-done(((f32[2304,1024]{1,0:T(8,128)}), f32[2304,256]{1,0:T(8,128)}) %reduce-scatter.3.cloned.1.call-update) | async-done | bytes 2359312 | tf_op jit(solution)/shard_map/reduce_scatter | solution.py:138
  (59 shorter events, 7.3 us)
Async XLA Ops:
  7.2 55.6 %copy-start = (bf16[1,1024,256]{2,1,0:T(8,128)(2,1)S(1)}, bf16[1,1024,256]{2,1,0:T(8,128)(2,1)}, u32[]{:S(2)}) copy-start(bf16[1,1024,256]{2,1,0:T(8,128)(2,1)} %param.9) | copy-start | bytes 1572868
  7.2 17.1 %copy-start.1 = (bf16[1,8,56,256]{3,2,1,0:T(8,128)(2,1)S(1)}, bf16[1,8,56,256]{3,2,1,0:T(8,128)(2,1)}, u32[]{:S(2)}) copy-start(bf16[1,8,56,256]{3,2,1,0:T(8,128)(2,1)} %param.6) | copy-start | bytes 688132
  9.6 14.8 %all-to-all-start = ((bf16[8,1,2]{2,1,0:T(2,128)(2,1)}), bf16[8,1,2]{2,1,0:T(2,128)(2,1)S(1)}, u32[]{:S(2)}, u32[]{:S(2)}) async-start(bf16[8,1,2]{2,1,0:T(2,128)(2,1)} %all_to_all.20), calls=%async_computation | async-start | bytes 8192 | tf_op jit(solution)/shard_map/all_to_all | solution.py:94
  15.6 8.2 %collective-permute-start = (bf16[1,56,256]{2,1,0:T(8,128)(2,1)S(1)}, bf16[1,56,256]{2,1,0:T(8,128)(2,1)S(1)}, u32[]{:S(2)}, u32[]{:S(2)}) collective-permute-start(bf16[1,56,256]{2,1,0:T(8,128)(2,1)S(1)} %get-tuple-element.6), channel_id=1, source_target_pairs={{0,4},{4,8},{8,12},{12,16},{16,20},{20,24},{24,28},{1,5},{5,9},{9,... | collective-permute-start | bytes 86024 | tf_op jit(solution)/shard_map/ppermute | solution.py:17
  19.1 5.2 %collective-permute-start.1 = (bf16[1,56,256]{2,1,0:T(8,128)(2,1)S(1)}, bf16[1,56,256]{2,1,0:T(8,128)(2,1)S(1)}, u32[]{:S(2)}, u32[]{:S(2)}) collective-permute-start(bf16[1,56,256]{2,1,0:T(8,128)(2,1)S(1)} %get-tuple-element.7), channel_id=1, source_target_pairs={{4,0},{8,4},{12,8},{16,12},{20,16},{24,20},{28,24},{5,1},{9,5},{13... | collective-permute-start | bytes 86024 | tf_op jit(solution)/shard_map/ppermute | solution.py:19
  24.4 10.5 %all-to-all-start.3 = ((bf16[8,2,16384]{2,1,0:T(2,128)(2,1)}), bf16[8,2,16384]{2,1,0:T(2,128)(2,1)S(1)}, u32[]{:S(2)}, u32[]{:S(2)}) async-start(bf16[8,2,16384]{2,1,0:T(2,128)(2,1)} %reshape.129), calls=%async_computation.3 | async-start | bytes 1048576 | tf_op jit(solution)/shard_map/all_to_all | solution.py:125
  34.9 15.9 %all-to-all-start.1 = ((bf16[8,2,25600]{2,1,0:T(2,128)(2,1)}), bf16[8,2,25600]{2,1,0:T(2,128)(2,1)S(1)}, u32[]{:S(2)}, u32[]{:S(2)}) async-start(bf16[8,2,25600]{2,1,0:T(2,128)(2,1)} %reshape.119), calls=%async_computation.1 | async-start | bytes 1638400 | tf_op jit(solution)/shard_map/all_to_all | solution.py:93
  41.4 53.5 %reduce-scatter.5.cloned.1.call-start = ((), (), s32[]{:S(2)}) async-start(), calls=%async_computation.7 | async-start | bytes 1310720 | tf_op jit(solution)/shard_map/reduce_scatter | solution.py:139
  52.0 0.7 copy-start.4
  52.7 8.4 %copy-start.2 = (bf16[10,8,8,2304]{3,2,1,0:T(8,128)(2,1)}, bf16[10,8,8,2304]{3,2,1,0:T(8,128)(2,1)S(1)}, u32[]{:S(2)}) copy-start(bf16[10,8,8,2304]{3,2,1,0:T(8,128)(2,1)S(1)} %slice_dynamic-update-slice_fusion) | copy-start | bytes 8847364
  62.7 192.3 %reduce-scatter.3.cloned.1.call-start = ((), (), s32[]{:S(2)}) async-start(), calls=%async_computation.6 | async-start | bytes 11796480 | tf_op jit(solution)/shard_map/reduce_scatter | solution.py:138
  62.8 3.0 %copy-start.3 = (bf16[10,8,8,2304]{3,2,1,0:T(8,128)(2,1)S(1)}, bf16[10,8,8,2304]{3,2,1,0:T(8,128)(2,1)}, u32[]{:S(2)}) copy-start(bf16[10,8,8,2304]{3,2,1,0:T(8,128)(2,1)} %copy-done.2) | copy-start | bytes 8847364
  72.2 9.2 %copy-start.5 = (u32[32]{0:T(128)S(1)}, u32[32]{0:T(128)}, u32[]{:S(2)}) copy-start(u32[32]{0:T(128)} %constant.33) | copy-start | bytes 388
  74.4 19.2 %all-to-all-start.2 = ((bf16[8,2,16384]{2,1,0:T(2,128)(2,1)}), bf16[8,2,16384]{2,1,0:T(2,128)(2,1)S(1)}, u32[]{:S(2)}, u32[]{:S(2)}) async-start(bf16[8,2,16384]{2,1,0:T(2,128)(2,1)} %reshape.124), calls=%async_computation.2 | async-start | bytes 1048576 | tf_op jit(solution)/shard_map/all_to_all | solution.py:118
Sparse Core Ops, SparseCore 0:
  62.8 29.4 reduce-scatter.4
  95.3 159.6 reduce-scatter.2
where the time goes:
time: 264 us; the launch traced here: 262 us
  waiting for transfers between devices  174 us (66%)
  starting transfers between devices  27.9 us (11%)
  matrix products  22.1 us (8%)
  between operations  15 us (6%)
  local copies, waits for them, and re-layouts  10.7 us (4%)
  blocking collectives  10.4 us (4%)
    reduce_scatter x1, waiting for transfers between devices, shards(): lax.psum_scatter(grad_first, 'dp', scatter_dimension=1, tiled=True)  160 us
    unnamed x1, blocking collectives  10.4 us
    dot_general x4, matrix products, contract_rows(): lax.dot_general(left_side, right_side, (((0,), (0,)), ((), ())), preferre...  8.52 us
    dot_general x1, matrix products, shards(): jnp.dot(patches, w_in[0], preferred_element_type=jnp.float32) + b_in[0]  8.39 us
    all_to_all x1, waiting for transfers between devices, shards(): lax.all_to_all(outgoing, 'expert', split_axis=0, concat_axis=0, tiled=True)  8.35 us
    all_to_all x1, starting transfers between devices, shards(): lax.all_to_all(result_slots, 'expert', split_axis=0, concat_axis=0, tiled...  6.92 us
    all_to_all x1, starting transfers between devices, shards(): lax.all_to_all(outgoing, 'expert', split_axis=0, concat_axis=0, tiled=True)  6.47 us
  transfers between devices with their start and end apart: 8, of which 4 were waited for; matrix products, arithmetic and copies ran while one was open for 8% of the time, Pallas kernels for 0%

commit v1 on v0

--- a/solution.py
+++ b/solution.py
@@ -89,12 +89,14 @@
         .astype(jnp.bfloat16)
         .reshape(owners, CAP, 64 * channels)
     )
-    arrived, occupied_in = (
-        lax.all_to_all(outgoing, "expert", split_axis=0, concat_axis=0, tiled=True),
-        lax.all_to_all(occupied, "expert", split_axis=0, concat_axis=0, tiled=True),
+    occupied_in = lax.all_to_all(occupied, "expert", split_axis=0, concat_axis=0, tiled=True)
+    arrived = lax.all_to_all(outgoing, "expert", split_axis=0, concat_axis=0, tiled=True)
+    target_in = lax.all_to_all(target_out, "expert", split_axis=0, concat_axis=0, tiled=True)
+    live_slots = occupied_in.reshape(slot_total).astype(jnp.float32)
+    slot_ids = jnp.arange(slot_total, dtype=jnp.int32)
+    position = jnp.sum(
+        jnp.where(slot_ids[None, :] < slot_ids[:, None], live_slots[None, :], 0.0), axis=1
     )
-    live_slots = occupied_in.reshape(slot_total).astype(jnp.float32)
-    position = jnp.cumsum(live_slots) - live_slots
     take_map = (
         (position[None, :] == jnp.arange(capacity, dtype=jnp.float32)[:, None])
         & (live_slots[None, :] > 0.5)
@@ -102,11 +104,22 @@
     compact = jnp.dot(
         take_map, arrived.reshape(slot_total, 100 * channels), preferred_element_type=jnp.float32
     ).astype(jnp.bfloat16)
+    target_rows = jnp.dot(
+        take_map, target_in.reshape(slot_total, 64 * channels), preferred_element_type=jnp.float32
+    ).astype(jnp.bfloat16)
+    packed = jnp.concatenate(
+        [
+            compact.reshape(capacity * 100, channels),
+            target_rows.reshape(capacity * 64, channels),
+        ],
+        axis=0,
+    )
+    gathered = lax.all_gather(packed, "dp", axis=0, tiled=False)
+    images = gathered.shape[0]
     compact = compact.reshape(capacity, 10, 10, channels)
     patches = unfold(compact)
     preact = jnp.dot(patches, w_in[0], preferred_element_type=jnp.float32) + b_in[0]
-    activation, gelu_slope = gelu_parts(preact)
-    hidden = activation.astype(jnp.bfloat16)
+    hidden = gelu_parts(preact)[0].astype(jnp.bfloat16)
     result = (
         jnp.dot(hidden, w_out[0], preferred_element_type=jnp.float32)
         .astype(jnp.bfloat16)
@@ -122,23 +135,25 @@
         .transpose(1, 0, 2, 3)
         .reshape(1, 8, columns, channels)
     )
-    target_in = lax.all_to_all(target_out, "expert", split_axis=0, concat_axis=0, tiled=True)
-    target_rows = jnp.dot(
-        take_map, target_in.reshape(slot_total, 64 * channels), preferred_element_type=jnp.float32
-    ).astype(jnp.bfloat16)
-    target_rows = target_rows.reshape(capacity * 64, channels)
-    grad_second = contract_rows(hidden, target_rows)
+    part = w_in.shape[2] // images
+    start = lax.axis_index("dp") * part
+    w_first = lax.dynamic_slice_in_dim(w_in[0], start, part, axis=1)
+    w_second = lax.dynamic_slice_in_dim(w_out[0], start, part, axis=0)
+    bias = lax.dynamic_slice_in_dim(b_in[0], start, part, axis=0)
+    all_patches = unfold(
+        gathered[:, : capacity * 100].reshape(images * capacity, 10, 10, channels)
+    )
+    all_targets = gathered[:, capacity * 100 :].reshape(images * capacity * 64, channels)
+    preact = jnp.dot(all_patches, w_first, preferred_element_type=jnp.float32) + bias
+    activation, gelu_slope = gelu_parts(preact)
+    hidden = activation.astype(jnp.bfloat16)
     back_hidden = lax.dot_general(
-        target_rows, w_out[0], (((1,), (1,)), ((), ())), preferred_element_type=jnp.float32
+        all_targets, w_second, (((1,), (1,)), ((), ())), preferred_element_type=jnp.float32
     )
     hidden_grad = (back_hidden * gelu_slope).astype(jnp.bfloat16)
+    grad_second = contract_rows(hidden, all_targets)
     grad_bias = jnp.sum(hidden_grad, axis=0, dtype=jnp.float32)
-    grad_first = contract_rows(patches, hidden_grad)
-    grad_first, grad_second, grad_bias = (
-        lax.psum_scatter(grad_first, "dp", scatter_dimension=1, tiled=True),
-        lax.psum_scatter(grad_second, "dp", scatter_dimension=0, tiled=True),
-        lax.psum_scatter(grad_bias, "dp", scatter_dimension=0, tiled=True),
-    )
+    grad_first = contract_rows(all_patches, hidden_grad)
     return (output, grad_first[None], grad_second[None], grad_bias[None])
 
 

time: 264 us -> 157 us (0.59)
  waiting for transfers between devices: 174 us -> 63.4 us
  local copies, waits for them, and re-layouts: 10.7 us -> 25 us
  blocking collectives: 10.4 us -> 0 us
    reduce_scatter x2 -> x0, waiting for transfers between devices: 160 us -> none  [the longest x1 160 us: shards(): lax.psum_scatter(grad_first, 'dp', scatter_dimension=1, tiled=True)]
    all_gather x0 -> x1, waiting for transfers between devices: none -> 42.5 us  [shards(): gathered = lax.all_gather(packed, 'dp', axis=0, tiled=False)]
    unnamed x1 -> x0, blocking collectives: 10.4 us -> none
    all_to_all x1, waiting for transfers between devices: 0.01 us -> 7.15 us  [shards(): lax.all_to_all(result_slots, 'expert', split_axis=0, concat_axis=0, tiled...]
    dot_general x1, matrix products: 0.51 us -> 6.93 us  [shards(): jnp.dot(hidden, w_out[0], preferred_element_type=jnp.float32)]
    unnamed x24 -> x30, local copies, waits for them, and re-layouts: 2.93 us -> 9.01 us
    dot_general x2, matrix products: 11.4 us -> 6.7 us  [the longest x1 4.7 us: shards(): jnp.dot(all_patches, w_first, preferred_element_type=jnp.float32) + bias]
    slice x0 -> x2, local copies, waits for them, and re-layouts: none -> 4.16 us  [the longest x1 2.46 us: shards(): gathered[:, capacity * 100:].reshape(images * capacity * 64, channels)]
  transfers between devices with their start and end apart: 8 -> 7, of which waited for: 4 -> 5; matrix products, arithmetic and copies ran while one was open for 8% -> 11% of each run, Pallas kernels for 0% -> 0%
where the time goes in v1:
time: 157 us; the launch traced here: 156 us
  waiting for transfers between devices  63.4 us (40%)
  starting transfers between devices  27.9 us (18%)
  local copies, waits for them, and re-layouts  25 us (16%)
  matrix products  22 us (14%)
  between operations  14.4 us (9%)
  other arithmetic  2.94 us (2%)
    all_gather x1, waiting for transfers between devices, shards(): gathered = lax.all_gather(packed, 'dp', axis=0, tiled=False)  42.5 us
    unnamed x30, local copies, waits for them, and re-layouts  9.01 us
    all_to_all x1, waiting for transfers between devices, shards(): lax.all_to_all(outgoing, 'expert', split_axis=0, concat_axis=0, tiled=True)  8.48 us
    all_to_all x1, waiting for transfers between devices, shards(): lax.all_to_all(result_slots, 'expert', split_axis=0, concat_axis=0, tiled...  7.15 us
    all_to_all x1, starting transfers between devices, shards(): lax.all_to_all(result_slots, 'expert', split_axis=0, concat_axis=0, tiled...  7 us
    dot_general x1, matrix products, shards(): jnp.dot(hidden, w_out[0], preferred_element_type=jnp.float32)  6.93 us
    dot_general x4, matrix products, contract_rows(): lax.dot_general(left_side, right_side, (((0,), (0,)), ((), ())), preferre...  6.69 us
    all_to_all x1, starting transfers between devices, shards(): lax.all_to_all(outgoing, 'expert', split_axis=0, concat_axis=0, tiled=True)  6.47 us
  transfers between devices with their start and end apart: 7, of which 5 were waited for; matrix products, arithmetic and copies ran while one was open for 11% of the time, Pallas kernels for 0%

profile of v1, /device:TPU:1, one launch (start us, length us, event | category | flops | bytes accessed | tf_op | source)
XLA Modules:
  0.0 155.6 jit_solution(12805241456888850222)
XLA Ops:
  9.6 5.2 %all-to-all-start = ((bf16[8,1,2]{2,1,0:T(2,128)(2,1)}), bf16[8,1,2]{2,1,0:T(2,128)(2,1)S(1)}, u32[]{:S(2)}, u32[]{:S(2)}) async-start(bf16[8,1,2]{2,1,0:T(2,128)(2,1)} %all_to_all.20), calls=%async_computation | async-start | bytes 8192 | tf_op jit(solution)/shard_map/all_to_all | solution.py:92
  15.6 3.5 %collective-permute-start = (bf16[1,56,256]{2,1,0:T(8,128)(2,1)S(1)}, bf16[1,56,256]{2,1,0:T(8,128)(2,1)S(1)}, u32[]{:S(2)}, u32[]{:S(2)}) collective-permute-start(bf16[1,56,256]{2,1,0:T(8,128)(2,1)S(1)} %get-tuple-element.6), channel_id=1, source_target_pairs={{0,4},{4,8},{8,12},{12,16},{16,20},{20,24},{24,28},{1,5},{5,9},{9,... | collective-permute-start | bytes 86024 | tf_op jit(solution)/shard_map/ppermute | solution.py:17
  19.1 1.9 %collective-permute-start.1 = (bf16[1,56,256]{2,1,0:T(8,128)(2,1)S(1)}, bf16[1,56,256]{2,1,0:T(8,128)(2,1)S(1)}, u32[]{:S(2)}, u32[]{:S(2)}) collective-permute-start(bf16[1,56,256]{2,1,0:T(8,128)(2,1)S(1)} %get-tuple-element.7), channel_id=1, source_target_pairs={{4,0},{8,4},{12,8},{16,12},{20,16},{24,20},{28,24},{5,1},{9,5},{13... | collective-permute-start | bytes 86024 | tf_op jit(solution)/shard_map/ppermute | solution.py:19
  22.6 1.1 reshape.110
  24.4 3.8 %all-to-all-start.3 = ((bf16[8,2,16384]{2,1,0:T(2,128)(2,1)}), bf16[8,2,16384]{2,1,0:T(2,128)(2,1)S(1)}, u32[]{:S(2)}, u32[]{:S(2)}) async-start(bf16[8,2,16384]{2,1,0:T(2,128)(2,1)} %reshape.110), calls=%async_computation.3 | async-start | bytes 1048576 | tf_op jit(solution)/shard_map/all_to_all | solution.py:94
  29.0 1.2 reshape.99
  30.2 4.7 %all-to-all-done.3 = bf16[8,2,16384]{2,1,0:T(2,128)(2,1)S(1)} async-done(((bf16[8,2,16384]{2,1,0:T(2,128)(2,1)}), bf16[8,2,16384]{2,1,0:T(2,128)(2,1)S(1)}, u32[]{:S(2)}, u32[]{:S(2)}) %all-to-all-start.3) | async-done | bytes 524320 | tf_op jit(solution)/shard_map/all_to_all | solution.py:94
  34.9 6.5 %all-to-all-start.1 = ((bf16[8,2,25600]{2,1,0:T(2,128)(2,1)}), bf16[8,2,25600]{2,1,0:T(2,128)(2,1)S(1)}, u32[]{:S(2)}, u32[]{:S(2)}) async-start(bf16[8,2,25600]{2,1,0:T(2,128)(2,1)} %reshape.99), calls=%async_computation.1 | async-start | bytes 1638400 | tf_op jit(solution)/shard_map/all_to_all | solution.py:93
  42.3 8.5 %all-to-all-done.1 = bf16[8,2,25600]{2,1,0:T(2,128)(2,1)S(1)} async-done(((bf16[8,2,25600]{2,1,0:T(2,128)(2,1)}), bf16[8,2,25600]{2,1,0:T(2,128)(2,1)S(1)}, u32[]{:S(2)}, u32[]{:S(2)}) %all-to-all-start.1) | async-done | bytes 819232 | tf_op jit(solution)/shard_map/all_to_all | solution.py:93
  54.5 1.6 %copy-done.4 = bf16[10,8,8,2304]{3,2,1,0:T(8,128)(2,1)} copy-done((bf16[10,8,8,2304]{3,2,1,0:T(8,128)(2,1)}, bf16[10,8,8,2304]{3,2,1,0:T(8,128)(2,1)S(1)}, u32[]{:S(2)}) %copy-start.4) | copy-done | bytes 2949144
  56.1 6.9 %convolution_convert_fusion.6 = bf16[640,256]{1,0:T(8,128)(2,1)S(1)} fusion(bf16[640,2304]{1,0:T(8,128)(2,1)} %bitcast.88, bf16[1,2304,1024]{2,1,0:T(8,128)(2,1)} %param.8, f32[1024]{0:T(1024)S(1)} %bitcast.90, bf16[1,1024,256]{2,1,0:T(8,128)(2,1)S(1)} %copy-done), kind=kOutput, calls=%fused_computation.31 | convolution fusion | flops 3359539200 | bytes 8523776 | tf_op jit(solution)/shard_map/dot_general | solution.py:124
  63.6 1.1 reshape.104
  64.8 7.0 %all-to-all-start.2 = ((bf16[8,2,16384]{2,1,0:T(2,128)(2,1)}), bf16[8,2,16384]{2,1,0:T(2,128)(2,1)S(1)}, u32[]{:S(2)}, u32[]{:S(2)}) async-start(bf16[8,2,16384]{2,1,0:T(2,128)(2,1)} %reshape.104), calls=%async_computation.2 | async-start | bytes 1048576 | tf_op jit(solution)/shard_map/all_to_all | solution.py:131
  71.8 7.2 %all-to-all-done.2 = bf16[8,2,16384]{2,1,0:T(2,128)(2,1)S(1)} async-done(((bf16[8,2,16384]{2,1,0:T(2,128)(2,1)}), bf16[8,2,16384]{2,1,0:T(2,128)(2,1)S(1)}, u32[]{:S(2)}, u32[]{:S(2)}) %all-to-all-start.2) | async-done | bytes 524320 | tf_op jit(solution)/shard_map/all_to_all | solution.py:131
  80.1 42.5 %all-gather.3.cloned.1.call-done = bf16[6560,256]{1,0:T(8,128)(2,1)} async-done(((bf16[1640,256]{1,0:T(8,128)(2,1)}), bf16[6560,256]{1,0:T(8,128)(2,1)}) %all-gather.3.cloned.1.call-update) | async-done | bytes 3358736 | tf_op jit(solution)/shard_map/all_gather | solution.py:117
  122.6 2.5 %slice.130 = bf16[4,640,256]{2,1,0:T(8,128)(2,1)} slice(bf16[4,1640,256]{2,1,0:T(8,128)(2,1)} %bitcast.78), slice={[0:4], [1000:1640], [0:256]} | slice | bytes 2621440 | tf_op jit(solution)/shard_map/slice | solution.py:146
  125.1 1.7 %slice.120 = bf16[4,1000,256]{2,1,0:T(8,128)(2,1)S(1)} slice(bf16[4,1640,256]{2,1,0:T(8,128)(2,1)} %bitcast.79), slice={[0:4], [0:1000], [0:256]} | slice | bytes 4096000 | tf_op jit(solution)/shard_map/slice | solution.py:144
  126.8 3.0 %reshape.113 = bf16[40,10,10,256]{3,2,1,0:T(8,128)(2,1)} reshape(bf16[4,1000,256]{2,1,0:T(8,128)(2,1)S(1)} %slice.120) | data formatting | bytes 4096000 | tf_op jit(solution)/shard_map/reshape | solution.py:144
  129.8 1.6 %slice_dynamic-update-slice_fusion.8 = bf16[40,8,8,2304]{3,2,1,0:T(8,128)(2,1)S(1)} fusion(bf16[40,10,10,256]{3,2,1,0:T(8,128)(2,1)} %reshape.113), kind=kLoop, calls=%fused_computation.30 | loop fusion | bytes 2621440
  131.4 2.2 %slice_dynamic-update-slice_fusion.7 = bf16[40,8,8,2304]{3,2,1,0:T(8,128)(2,1)S(1)} fusion(bf16[40,8,8,2304]{3,2,1,0:T(8,128)(2,1)S(1)} %slice_dynamic-update-slice_fusion.8, bf16[40,10,10,256]{3,2,1,0:T(8,128)(2,1)} %reshape.113), kind=kLoop, calls=%fused_computation.29 | loop fusion | bytes 2621440
  136.0 4.7 %convolution_add_fusion = f32[2560,256]{1,0:T(8,128)S(1)} fusion(bf16[2560,2304]{1,0:T(8,128)(2,1)S(1)} %bitcast.86, f32[256]{0:T(256)S(1)} %bitcast.89, bf16[1,2304,1024]{2,1,0:T(8,128)(2,1)} %param.8, s32[]{:T(128)S(6)} %select_n.10), kind=kOutput, calls=%fused_computation.12 | convolution fusion | flops 3020554240 | bytes 15598596 | tf_op jit(solution)/shard_map/dot_general | solution.py:147
  140.7 1.4 fusion.12
  142.1 2.0 %convert_reduce_fusion = (f32[256]{0:T(256)}, bf16[2560,256]{1,0:T(8,128)(2,1)S(1)}) fusion(f32[2560,256]{1,0:T(8,128)S(1)} %convolution_add_fusion, bf16[2560,256]{1,0:T(8,128)(2,1)S(1)} %bitcast.82, bf16[1,1024,256]{2,1,0:T(8,128)(2,1)S(1)} %copy-done, s32[]{:T(128)S(6)} %select_n.10), kind=kOutput, calls=%fused_computation.17 | convolution fusion | flops 343408384 | bytes 5374980 | tf_op jit(solution)/shard_map/dot_general | solution.py:150
  144.1 4.7 %convolution_bitcast_fusion = f32[1,2304,256]{2,1,0:T(8,128)} fusion(bf16[2560,2304]{1,0:T(8,128)(2,1)S(1)} %bitcast.87, bf16[2560,256]{1,0:T(8,128)(2,1)S(1)} %get-tuple-element.9), kind=kOutput, calls=%fused_computation.9 | convolution fusion | flops 3019898880 | bytes 15466496 | tf_op jit(solution)/shard_map/dot_general | solution.py:44
  (64 shorter events, 14.8 us)
Async XLA Ops:
  7.2 49.0 %copy-start = (bf16[1,1024,256]{2,1,0:T(8,128)(2,1)S(1)}, bf16[1,1024,256]{2,1,0:T(8,128)(2,1)}, u32[]{:S(2)}) copy-start(bf16[1,1024,256]{2,1,0:T(8,128)(2,1)} %param.9) | copy-start | bytes 1572868
  7.2 17.1 %copy-start.3 = (bf16[1,8,56,256]{3,2,1,0:T(8,128)(2,1)S(1)}, bf16[1,8,56,256]{3,2,1,0:T(8,128)(2,1)}, u32[]{:S(2)}) copy-start(bf16[1,8,56,256]{3,2,1,0:T(8,128)(2,1)} %param.6) | copy-start | bytes 688132
  9.6 14.8 %all-to-all-start = ((bf16[8,1,2]{2,1,0:T(2,128)(2,1)}), bf16[8,1,2]{2,1,0:T(2,128)(2,1)S(1)}, u32[]{:S(2)}, u32[]{:S(2)}) async-start(bf16[8,1,2]{2,1,0:T(2,128)(2,1)} %all_to_all.20), calls=%async_computation | async-start | bytes 8192 | tf_op jit(solution)/shard_map/all_to_all | solution.py:92
  15.6 8.2 %collective-permute-start = (bf16[1,56,256]{2,1,0:T(8,128)(2,1)S(1)}, bf16[1,56,256]{2,1,0:T(8,128)(2,1)S(1)}, u32[]{:S(2)}, u32[]{:S(2)}) collective-permute-start(bf16[1,56,256]{2,1,0:T(8,128)(2,1)S(1)} %get-tuple-element.6), channel_id=1, source_target_pairs={{0,4},{4,8},{8,12},{12,16},{16,20},{20,24},{24,28},{1,5},{5,9},{9,... | collective-permute-start | bytes 86024 | tf_op jit(solution)/shard_map/ppermute | solution.py:17
  19.1 5.2 %collective-permute-start.1 = (bf16[1,56,256]{2,1,0:T(8,128)(2,1)S(1)}, bf16[1,56,256]{2,1,0:T(8,128)(2,1)S(1)}, u32[]{:S(2)}, u32[]{:S(2)}) collective-permute-start(bf16[1,56,256]{2,1,0:T(8,128)(2,1)S(1)} %get-tuple-element.7), channel_id=1, source_target_pairs={{4,0},{8,4},{12,8},{16,12},{20,16},{24,20},{28,24},{5,1},{9,5},{13... | collective-permute-start | bytes 86024 | tf_op jit(solution)/shard_map/ppermute | solution.py:19
  24.4 10.5 %all-to-all-start.3 = ((bf16[8,2,16384]{2,1,0:T(2,128)(2,1)}), bf16[8,2,16384]{2,1,0:T(2,128)(2,1)S(1)}, u32[]{:S(2)}, u32[]{:S(2)}) async-start(bf16[8,2,16384]{2,1,0:T(2,128)(2,1)} %reshape.110), calls=%async_computation.3 | async-start | bytes 1048576 | tf_op jit(solution)/shard_map/all_to_all | solution.py:94
  34.9 15.9 %all-to-all-start.1 = ((bf16[8,2,25600]{2,1,0:T(2,128)(2,1)}), bf16[8,2,25600]{2,1,0:T(2,128)(2,1)S(1)}, u32[]{:S(2)}, u32[]{:S(2)}) async-start(bf16[8,2,25600]{2,1,0:T(2,128)(2,1)} %reshape.99), calls=%async_computation.1 | async-start | bytes 1638400 | tf_op jit(solution)/shard_map/all_to_all | solution.py:93
  41.4 81.3 %all-gather.3.cloned.1.call-start = ((), (), s32[]{:S(2)}) async-start(), calls=%async_computation.4 | async-start | bytes 4198400 | tf_op jit(solution)/shard_map/all_gather | solution.py:117
  53.7 2.4 %copy-start.5 = (f32[1,1024]{1,0:T(1,128)S(1)}, f32[1,1024]{1,0:T(1,128)}, u32[]{:S(2)}) copy-start(f32[1,1024]{1,0:T(1,128)} %param.10) | copy-start | bytes 12292
  54.5 1.6 %copy-start.4 = (bf16[10,8,8,2304]{3,2,1,0:T(8,128)(2,1)}, bf16[10,8,8,2304]{3,2,1,0:T(8,128)(2,1)S(1)}, u32[]{:S(2)}) copy-start(bf16[10,8,8,2304]{3,2,1,0:T(8,128)(2,1)S(1)} %slice_dynamic-update-slice_fusion.9) | copy-start | bytes 8847364
  64.8 14.2 %all-to-all-start.2 = ((bf16[8,2,16384]{2,1,0:T(2,128)(2,1)}), bf16[8,2,16384]{2,1,0:T(2,128)(2,1)S(1)}, u32[]{:S(2)}, u32[]{:S(2)}) async-start(bf16[8,2,16384]{2,1,0:T(2,128)(2,1)} %reshape.104), calls=%async_computation.2 | async-start | bytes 1048576 | tf_op jit(solution)/shard_map/all_to_all | solution.py:131
  129.8 3.8 %copy-start.1 = (bf16[40,10,10,256]{3,2,1,0:T(8,128)(2,1)S(1)}, bf16[40,10,10,256]{3,2,1,0:T(8,128)(2,1)}, u32[]{:S(2)}) copy-start(bf16[40,10,10,256]{3,2,1,0:T(8,128)(2,1)} %reshape.113) | copy-start | bytes 6144004
  135.9 4.7 %copy-start.2 = (bf16[4,640,256]{2,1,0:T(8,128)(2,1)S(1)}, bf16[4,640,256]{2,1,0:T(8,128)(2,1)}, u32[]{:S(2)}) copy-start(bf16[4,640,256]{2,1,0:T(8,128)(2,1)} %slice.130) | copy-start | bytes 3932164
Sparse Core Ops, SparseCore 0:
  53.4 69.2 all-gather.2

commit v2 on v0

v2 whole, which is shorter than its diff:
```python
import functools

import jax
import jax.numpy as jnp
from jax import lax
from jax.experimental import pallas as pl
from jax.experimental.pallas import tpu as pltpu
from jax.sharding import PartitionSpec as P

CAP = 2
SLOT = 176
FRAME = SLOT - 64
MESH = pl.DeviceIdType.MESH


def extended(cells):
    count = lax.axis_size("expert")
    ends = count - 1
    return jnp.concatenate(
        [
            lax.ppermute(cells[-1:], "expert", [(i, i + 1) for i in range(ends)]),
            cells,
            lax.ppermute(cells[:1], "expert", [(i + 1, i) for i in range(ends)]),
        ],
        axis=0,
    )


def gelu_parts(preact):
    normal_cdf = 0.5 * (1.0 + lax.erf(preact * 0.7071067811865476))
    density = jnp.exp(-0.5 * preact * preact) * 0.3989422804014327
    return (preact * normal_cdf, normal_cdf + preact * density)


def contract_rows(left_side, right_side):
    return lax.dot_general(
        left_side, right_side, (((0,), (0,)), ((), ())), preferred_element_type=jnp.float32
    )


def kernel(
    owners,
    images,
    batch,
    send_src,
    take_src,
    back_src,
    mine_src,
    tiles,
    pick,
    w_in,
    w_out,
    b_in,
    out_ref,
    first_ref,
    second_ref,
    bias_ref,
    leaving,
    arrived,
    held,
    patches,
    result,
    going,
    returned,
    send_a,
    recv_a,
    send_b,
    recv_b,
    send_right,
    send_left,
    recv_z,
):
    me = lax.axis_index("expert")
    z = lax.axis_index("dp")
    tile_count = out_ref.shape[0]
    capacity = held.shape[1]
    batches = capacity // batch
    slot_total = owners * CAP
    channels = tiles.shape[2]
    part = w_in.shape[1] // images
    has_right = z < images - 1
    has_left = z > 0

    def peer(step):
        return lax.rem(me + step, owners)

    barrier = pltpu.get_barrier_semaphore()

    @pl.loop(1, owners)
    def _(step):
        pl.semaphore_signal(barrier, inc=1, device_id=(peer(step), z), device_id_type=MESH)

    @pl.when(has_right)
    def _():
        pl.semaphore_signal(barrier, inc=1, device_id=(me, z + 1), device_id_type=MESH)

    @pl.when(has_left)
    def _():
        pl.semaphore_signal(barrier, inc=1, device_id=(me, z - 1), device_id_type=MESH)

    @pl.loop(0, slot_total)
    def _(slot):
        leaving[slot] = tiles[send_src[slot]]

    arrived[slot_total] = jnp.zeros_like(arrived[slot_total])
    first_ref[...] = jnp.zeros_like(first_ref)
    second_ref[...] = jnp.zeros_like(second_ref)
    bias_ref[...] = jnp.zeros_like(bias_ref)
    arrived[pl.ds(me * CAP, CAP)] = leaving[pl.ds(me * CAP, CAP)]

    beside = has_right.astype(jnp.int32) + has_left.astype(jnp.int32)
    pl.semaphore_wait(barrier, owners - 1 + beside)

    def route(source, target, send_sem, recv_sem, to, origin):
        return pltpu.make_async_remote_copy(
            src_ref=source.at[pl.ds(to * CAP, CAP)],
            dst_ref=target.at[pl.ds(origin * CAP, CAP)],
            send_sem=send_sem.at[to],
            recv_sem=recv_sem.at[origin],
            device_id=(to, z),
            device_id_type=MESH,
        )

    @pl.loop(1, owners)
    def _(step):
        route(leaving, arrived, send_a, recv_a, peer(step), me).start()

    @pl.loop(1, owners)
    def _(step):
        other = peer(owners - step)
        route(leaving, arrived, send_a, recv_a, other, other).wait_recv()

    def relay(image, part_at, send_sem, to):
        span = held.at[image, pl.ds(part_at * batch, batch)]
        return pltpu.make_async_remote_copy(
            src_ref=span,
            dst_ref=span,
            send_sem=send_sem.at[image, part_at],
            recv_sem=recv_z.at[image, part_at],
            device_id=(me, to),
            device_id_type=MESH,
        )

    def to_right(image, part_at):
        return relay(image, part_at, send_right, z + 1)

    def to_left(image, part_at):
        return relay(image, part_at, send_left, z - 1)

    @pl.loop(0, batches)
    def _(part_at):
        @pl.loop(0, batch)
        def _(within):
            tile = part_at * batch + within
            held[z, tile] = arrived[take_src[tile]]

        @pl.when(has_right)
        def _():
            to_right(z, part_at).start()

        @pl.when(has_left)
        def _():
            to_left(z, part_at).start()

    def unfold(image, part_at):
        for within in range(batch):
            frame = held[image, part_at * batch + within, 64:SLOT, :]
            for shift in range(9):
                patches[within * 64 : (within + 1) * 64, shift * channels : (shift + 1) * channels] = jnp.dot(
                    pick[shift * 64 : (shift + 1) * 64, :], frame, preferred_element_type=jnp.float32
                ).astype(jnp.bfloat16)

    def columns(block):
        return pl.ds(pl.multiple_of(block * part, part), part)

    def preact_of(block):
        return (
            jnp.dot(patches[...], w_in[:, columns(block)], preferred_element_type=jnp.float32)
            + b_in[pl.ds(block, 1), :]
        )

    def gradients(image, part_at):
        activation, slope = gelu_parts(preact_of(z))
        hidden = activation.astype(jnp.bfloat16)
        target = held[image, pl.ds(part_at * batch, batch), 0:64, :].reshape(batch * 64, channels)
        back = lax.dot_general(
            target,
            w_out[columns(z), :],
            (((1,), (1,)), ((), ())),
            preferred_element_type=jnp.float32,
        )
        hidden_grad = (back * slope).astype(jnp.bfloat16)
        second_ref[...] += contract_rows(hidden, target)
        bias_ref[...] += jnp.sum(hidden_grad.astype(jnp.float32), axis=0, keepdims=True)
        first_ref[...] += contract_rows(hidden_grad, patches[...])

    @pl.loop(0, batches)
    def _(part_at):
        unfold(z, part_at)

        def add(block, total):
            hidden = gelu_parts(preact_of(block))[0].astype(jnp.bfloat16)
            return total + jnp.dot(
                hidden, w_out[columns(block), :], preferred_element_type=jnp.float32
            )

        total = lax.fori_loop(
            0, images, add, jnp.zeros((batch * 64, channels), jnp.float32)
        )
        result[pl.ds(part_at * batch, batch)] = total.astype(jnp.bfloat16).reshape(
            batch, 64, channels
        )

    @pl.loop(0, slot_total)
    def _(slot):
        going[slot] = result[back_src[slot]]

    returned[pl.ds(me * CAP, CAP)] = going[pl.ds(me * CAP, CAP)]

    @pl.loop(1, owners)
    def _(step):
        route(going, returned, send_b, recv_b, peer(step), me).start()

    @pl.loop(0, images * batches)
    def _(index):
        distance = index // batches
        part_at = lax.rem(index, batches)
        low = z - distance
        high = z + distance
        arrives_low = (distance > 0) & (low >= 0)
        arrives_high = (distance > 0) & (high < images)

        @pl.when(arrives_low)
        def _():
            relay(low, part_at, send_right, z).wait_recv()

            @pl.when(has_right)
            def _():
                to_right(low, part_at).start()

        @pl.when(arrives_high)
        def _():
            relay(high, part_at, send_left, z).wait_recv()

            @pl.when(has_left)
            def _():
                to_left(high, part_at).start()

        @pl.loop(0, 2)
        def _(side):
            image = jnp.where(side == 0, low, high)

            @pl.when((image >= 0) & (image < images) & ((distance > 0) | (side == 0)))
            def _():
                unfold(image, part_at)
                gradients(image, part_at)

    @pl.loop(1, owners)
    def _(step):
        other = peer(owners - step)
        route(going, returned, send_b, recv_b, other, other).wait_recv()

    @pl.loop(0, tile_count)
    def _(tile):
        out_ref[tile] = returned[mine_src[tile]]

    @pl.loop(1, owners)
    def _(step):
        other = peer(step)
        route(leaving, arrived, send_a, recv_a, other, me).wait_send()
        route(going, returned, send_b, recv_b, other, me).wait_send()

    @pl.loop(0, images * batches)
    def _(index):
        image = index // batches
        part_at = lax.rem(index, batches)

        @pl.when(has_right & (image <= z))
        def _():
            to_right(image, part_at).wait_send()

        @pl.when(has_left & (image >= z))
        def _():
            to_left(image, part_at).wait_send()


def pick_matrix():
    row = jnp.arange(9 * 64, dtype=jnp.int32)
    shift = row // 64
    cell = row % 64
    wanted = (cell // 8 + shift // 3) * 10 + cell % 8 + shift % 3
    return (wanted[:, None] == jnp.arange(FRAME, dtype=jnp.int32)[None, :]).astype(jnp.bfloat16)


def shards(heatmap, labels, w_in, w_out, b_in, cotangent):
    channels = heatmap.shape[3]
    columns = heatmap.shape[2]
    tile_count = columns // 8
    owners = lax.axis_size("expert")
    images = lax.axis_size("dp")
    slot_total = owners * CAP
    capacity = 3 * tile_count // 2
    batch = max(b for b in range(1, 8) if capacity % b == 0)
    hidden_size = w_in.shape[2]
    part = hidden_size // images
    every = lax.all_gather(labels[0], "expert", axis=0, tiled=False)
    bordered = extended(heatmap[0])
    bordered = jnp.pad(bordered, ((0, 0), (1, 7), (0, 0)))
    left_part = bordered[:, :columns].reshape(10, tile_count, 8, channels)
    right_part = bordered[:, 8 : columns + 8].reshape(10, tile_count, 8, channels)[:, :, :2]
    framed = (
        jnp.concatenate([left_part, right_part], axis=2)
        .transpose(1, 0, 2, 3)
        .reshape(tile_count, 100, channels)
    )
    targets = (
        cotangent[0]
        .reshape(8, tile_count, 8, channels)
        .transpose(1, 0, 2, 3)
        .reshape(tile_count, 64, channels)
    )
    tiles = jnp.concatenate([targets, framed], axis=1)
    tiles = jnp.pad(tiles, ((0, 1), (0, SLOT - 164), (0, 0)))

    labels_here = labels[0]
    tile_ids = jnp.arange(tile_count, dtype=jnp.int32)
    earlier = (labels_here[None, :] == labels_here[:, None]) & (
        tile_ids[None, :] < tile_ids[:, None]
    )
    slot_index = labels_here * CAP + jnp.sum(earlier.astype(jnp.int32), axis=1)
    slot_ids = jnp.arange(slot_total, dtype=jnp.int32)
    send_src = tile_count + jnp.sum(
        jnp.where(
            slot_index[None, :] == slot_ids[:, None], tile_ids[None, :] - tile_count, 0
        ),
        axis=1,
    )
    counts = jnp.sum((every == lax.axis_index("expert")).astype(jnp.int32), axis=1)
    live = (slot_ids % CAP) < jnp.broadcast_to(counts[:, None], (owners, CAP)).reshape(slot_total)
    position = jnp.sum(
        ((slot_ids[None, :] < slot_ids[:, None]) & live[None, :]).astype(jnp.int32), axis=1
    )
    places = jnp.arange(capacity, dtype=jnp.int32)
    take_src = slot_total + jnp.sum(
        jnp.where(
            (position[None, :] == places[:, None]) & live[None, :],
            slot_ids[None, :] - slot_total,
            0,
        ),
        axis=1,
    )
    back_src = jnp.minimum(position, capacity - 1)

    smem = pl.BlockSpec(memory_space=pltpu.SMEM)
    vmem = pl.BlockSpec(memory_space=pltpu.VMEM)
    bf16 = jnp.bfloat16
    dma = pltpu.SemaphoreType.DMA
    batches = capacity // batch
    out, first, second, bias = pl.pallas_call(
        functools.partial(kernel, owners, images, batch),
        out_shape=(
            jax.ShapeDtypeStruct((tile_count, 64, channels), bf16),
            jax.ShapeDtypeStruct((part, 9 * channels), jnp.float32),
            jax.ShapeDtypeStruct((part, channels), jnp.float32),
            jax.ShapeDtypeStruct((1, part), jnp.float32),
        ),
        in_specs=[smem] * 4 + [vmem] * 5,
        out_specs=(vmem,) * 4,
        scratch_shapes=[
            pltpu.VMEM((slot_total, SLOT, channels), bf16),
            pltpu.VMEM((slot_total + 1, SLOT, channels), bf16),
            pltpu.VMEM((images, capacity, SLOT, channels), bf16),
            pltpu.VMEM((batch * 64, 9 * channels), bf16),
            pltpu.VMEM((capacity, 64, channels), bf16),
            pltpu.VMEM((slot_total, 64, channels), bf16),
            pltpu.VMEM((slot_total, 64, channels), bf16),
            dma((owners,)),
            dma((owners,)),
            dma((owners,)),
            dma((owners,)),
            dma((images, batches)),
            dma((images, batches)),
            dma((images, batches)),
        ],
        compiler_params=pltpu.CompilerParams(
            collective_id=0, has_side_effects=True, vmem_limit_bytes=60 * 2**20
        ),
    )(
        send_src,
        take_src,
        back_src,
        slot_index,
        tiles,
        pick_matrix(),
        w_in[0],
        w_out[0],
        b_in[0].reshape(images, part),
    )
    output = (
        out.reshape(tile_count, 8, 8, channels)
        .transpose(1, 0, 2, 3)
        .reshape(1, 8, columns, channels)
    )
    return (output, first.T[None], second[None], bias)


def solution(mesh):
    return jax.shard_map(
        shards,
        mesh=mesh,
        in_specs=(
            P("dp", "expert", None, None),
            P("dp", "expert"),
            P("expert", None, None),
            P("expert", None, None),
            P("expert", None),
            P("dp", "expert", None, None),
        ),
        out_specs=(
            P("dp", "expert", None, None),
            P("expert", None, "dp"),
            P("expert", "dp", None),
            P("expert", "dp"),
        ),
        check_vma=False,
    )
```

time: 264 us -> 118 us (0.45)
  waiting for transfers between devices: 174 us -> 0.01 us
  Pallas kernels: 0 us -> 83.7 us
  matrix products: 22.1 us -> 0 us
  starting transfers between devices: 27.9 us -> 6.42 us
  between operations: 15 us -> 0.75 us
  other arithmetic: 2.04 us -> 8.6 us
    reduce_scatter x2 -> x0, waiting for transfers between devices: 160 us -> none  [the longest x1 160 us: shards(): lax.psum_scatter(grad_first, 'dp', scatter_dimension=1, tiled=True)]
    pallas_call x0 -> x1, Pallas kernels: none -> 83.7 us  [shards(): pl.pallas_call(functools.partial(kernel, owners, images, batch), out_shap...]
    all_to_all x4 -> x0, starting transfers between devices: 22.4 us -> none  [the longest x1 6.92 us: shards(): lax.all_to_all(result_slots, 'expert', split_axis=0, concat_axis=0, tiled...]
    dot_general x11 -> x0, matrix products: 22.1 us -> none  [the longest x4 8.52 us: contract_rows(): lax.dot_general(left_side, right_side, (((0,), (0,)), ((), ())), preferre...]
    all_to_all x4 -> x0, waiting for transfers between devices: 13 us -> none  [the longest x1 8.35 us: shards(): lax.all_to_all(outgoing, 'expert', split_axis=0, concat_axis=0, tiled=True)]
    unnamed x1 -> x0, blocking collectives: 10.4 us -> none
    all_gather x0 -> x1, blocking collectives: none -> 10.1 us  [shards(): every = lax.all_gather(labels[0], 'expert', axis=0, tiled=False)]
    reshape x10 -> x4, local copies, waits for them, and re-layouts: 5.84 us -> 1.81 us  [the longest x1 1.64 us: shards(): output = out.reshape(tile_count, 8, 8, channels).transpose(1, 0, 2, 3).re...]
  transfers between devices with their start and end apart: 8 -> 2, of which waited for: 4 -> 0; matrix products, arithmetic and copies ran while one was open for 8% -> 7% of each run, Pallas kernels for 0% -> 0%
where the time goes in v2:
time: 118 us
  Pallas kernels  83.7 us (71%)
  blocking collectives  10.1 us (9%)
  other arithmetic  8.6 us (7%)
  local copies, waits for them, and re-layouts  8.34 us (7%)
  starting transfers between devices  6.42 us (5%)
    pallas_call x1, Pallas kernels, shards(): pl.pallas_call(functools.partial(kernel, owners, images, batch), out_shap...  83.7 us
    all_gather x1, blocking collectives, shards(): every = lax.all_gather(labels[0], 'expert', axis=0, tiled=False)  10.1 us
    unnamed x11, local copies, waits for them, and re-layouts  4.89 us
    ppermute x1, starting transfers between devices, extended(): lax.ppermute(cells[-1:], 'expert', [(i, i + 1) for i in range(ends)])  4.5 us
  transfers between devices with their start and end apart: 2, of which 0 were waited for; matrix products, arithmetic and copies ran while one was open for 7% of the time, Pallas kernels for 0%

profile of v2, /device:TPU:1, one launch (start us, length us, event | category | flops | bytes accessed | tf_op | source)
XLA Modules:
  0.0 118.0 jit_solution(13976991729099947703)
XLA Ops:
  0.6 0.8 slice_bitcast_fusion.3
  1.5 4.5 %collective-permute-start = (bf16[1,56,256]{2,1,0:T(8,128)(2,1)S(1)}, bf16[1,56,256]{2,1,0:T(8,128)(2,1)S(1)}, u32[]{:S(2)}, u32[]{:S(2)}) collective-permute-start(bf16[1,56,256]{2,1,0:T(8,128)(2,1)S(1)} %get-tuple-element.30), channel_id=1, source_target_pairs={{0,4},{4,8},{8,12},{12,16},{16,20},{20,24},{24,28},{1,5},{5,9},{9,... | collective-permute-start | bytes 86024 | tf_op jit(solution)/shard_map/ppermute | solution.py:21
  6.0 1.9 %collective-permute-start.1 = (bf16[1,56,256]{2,1,0:T(8,128)(2,1)S(1)}, bf16[1,56,256]{2,1,0:T(8,128)(2,1)S(1)}, u32[]{:S(2)}, u32[]{:S(2)}) collective-permute-start(bf16[1,56,256]{2,1,0:T(8,128)(2,1)S(1)} %get-tuple-element.31), channel_id=1, source_target_pairs={{4,0},{8,4},{12,8},{16,12},{20,16},{24,20},{28,24},{5,1},{9,5},{13... | collective-permute-start | bytes 86024 | tf_op jit(solution)/shard_map/ppermute | solution.py:23
  7.9 0.9 convert_reduce_fusion.1
  8.8 1.2 multiply_add_fusion.mine_src
  10.0 0.7 fusion.44
  10.7 10.1 %all-gather = s32[8,1,7]{2,1,0:T(1,128)S(1)} all-gather(s32[1,1,7]{2,1,0:T(1,128)} %bitcast.48), channel_id=1, replica_groups=mesh['expert'=8,'dp'=4] {'expert'}, dimensions={0}, use_global_device_ids=true | all-gather | bytes 252 | tf_op jit(solution)/shard_map/all_gather | solution.py:306
  20.8 0.2 fusion.35
  21.2 0.1 convert_reduce_fusion
  21.3 0.1 select_reduce_fusion.1
  21.4 0.1 select_reduce_fusion
  21.5 0.5 broadcast_minimum_fusion
  22.0 0.8 fusion.12.pick
  22.9 0.6 broadcast_add_fusion.take_src
  23.4 0.5 broadcast.241
  23.9 1.3 %reduce.4 = f32[1024]{0:T(1024)S(1)} reduce(f32[1,1024]{1,0:T(1,128)} %param.10, f32[]{:T(128)} %broadcast.241), dimensions={0}, to_apply=%param.10.reduce_sub_computation.3 | reduce | bytes 8196 | tf_op args[4]
  25.3 0.6 reshape_squeeze.7.b_in
  25.9 1.0 fusion.11
  27.3 0.9 fusion.5.tiles
  28.2 83.7 %shard_map.93 = (bf16[7,64,256]{2,1,0:T(8,128)(2,1)}, f32[256,2304]{1,0:T(8,128)}, f32[256,256]{1,0:T(8,128)}, f32[1,256]{1,0:T(1,128)}) custom-call(s32[16]{0:T(128)} %get-tuple-element.33.send_src, s32[10]{0:T(128)} %broadcast_add_fusion.take_src, s32[16]{0:T(128)} %get-tuple-element.32.back_src, s32[7]{0:T(128)} %multiply_add_fusion.mine_src, ...), custom_call_target="tpu_custom_call" | custom-call | tf_op jit(solution)/shard_map/pallas_call | solution.py:359
  112.0 1.6 %copy_bitcast_fusion = bf16[1,8,56,256]{3,2,1,0:T(8,128)(2,1)} fusion(bf16[7,64,256]{2,1,0:T(8,128)(2,1)} %get-tuple-element.8), kind=kLoop, calls=%fused_computation.21 | loop fusion | bytes 458752 | tf_op jit(solution)/shard_map/reshape | solution.py:402
  113.6 3.1 %copy.32 = f32[1,2304,256]{2,1,0:T(8,128)} copy(f32[1,2304,256]{1,2,0:T(8,128)} %bitcast.42) | data formatting | bytes 4718592
  116.7 0.7 copy.38
  117.4 0.6 copy.39
  (21 shorter events, 0.5 us)
Async XLA Ops:
  0.6 22.2 %copy-start = (bf16[1,8,56,256]{3,2,1,0:T(8,128)(2,1)S(1)}, bf16[1,8,56,256]{3,2,1,0:T(8,128)(2,1)}, u32[]{:S(2)}) copy-start(bf16[1,8,56,256]{3,2,1,0:T(8,128)(2,1)} %param.11) | copy-start | bytes 688132
  1.5 24.4 %collective-permute-start = (bf16[1,56,256]{2,1,0:T(8,128)(2,1)S(1)}, bf16[1,56,256]{2,1,0:T(8,128)(2,1)S(1)}, u32[]{:S(2)}, u32[]{:S(2)}) collective-permute-start(bf16[1,56,256]{2,1,0:T(8,128)(2,1)S(1)} %get-tuple-element.30), channel_id=1, source_target_pairs={{0,4},{4,8},{8,12},{12,16},{16,20},{20,24},{24,28},{1,5},{5,9},{9,... | collective-permute-start | bytes 86024 | tf_op jit(solution)/shard_map/ppermute | solution.py:21
  6.0 19.9 %collective-permute-start.1 = (bf16[1,56,256]{2,1,0:T(8,128)(2,1)S(1)}, bf16[1,56,256]{2,1,0:T(8,128)(2,1)S(1)}, u32[]{:S(2)}, u32[]{:S(2)}) collective-permute-start(bf16[1,56,256]{2,1,0:T(8,128)(2,1)S(1)} %get-tuple-element.31), channel_id=1, source_target_pairs={{4,0},{8,4},{12,8},{16,12},{20,16},{24,20},{28,24},{5,1},{9,5},{13... | collective-permute-start | bytes 86024 | tf_op jit(solution)/shard_map/ppermute | solution.py:23
  113.6 3.1 %copy-start.1 = (f32[256,256]{1,0:T(8,128)S(1)}, f32[256,256]{1,0:T(8,128)}, u32[]{:S(2)}) copy-start(f32[256,256]{1,0:T(8,128)} %get-tuple-element.10) | copy-start | bytes 786436
  113.6 3.8 %copy-start.2 = (f32[1,256]{1,0:T(1,128)S(1)}, f32[1,256]{1,0:T(1,128)}, u32[]{:S(2)}) copy-start(f32[1,256]{1,0:T(1,128)} %get-tuple-element.41) | copy-start | bytes 3076

commit v3 on v2

--- a/solution.py
+++ b/solution.py
@@ -8,8 +8,7 @@
 from jax.sharding import PartitionSpec as P
 
 CAP = 2
-SLOT = 176
-FRAME = SLOT - 64
+FRAME = 112
 MESH = pl.DeviceIdType.MESH
 
 
@@ -46,8 +45,8 @@
     take_src,
     back_src,
     mine_src,
-    tiles,
-    pick,
+    targets,
+    frames,
     w_in,
     w_out,
     b_in,
@@ -55,17 +54,23 @@
     first_ref,
     second_ref,
     bias_ref,
-    leaving,
-    arrived,
-    held,
+    leaving_t,
+    leaving_f,
+    arrived_t,
+    arrived_f,
+    held_t,
+    held_f,
+    pick,
     patches,
     result,
     going,
     returned,
-    send_a,
-    recv_a,
-    send_b,
-    recv_b,
+    send_t,
+    recv_t,
+    send_f,
+    recv_f,
+    send_o,
+    recv_o,
     send_right,
     send_left,
     recv_z,
@@ -73,10 +78,10 @@
     me = lax.axis_index("expert")
     z = lax.axis_index("dp")
     tile_count = out_ref.shape[0]
-    capacity = held.shape[1]
+    capacity = held_t.shape[1]
     batches = capacity // batch
     slot_total = owners * CAP
-    channels = tiles.shape[2]
+    channels = targets.shape[2]
     part = w_in.shape[1] // images
     has_right = z < images - 1
     has_left = z > 0
@@ -100,13 +105,14 @@
 
     @pl.loop(0, slot_total)
     def _(slot):
-        leaving[slot] = tiles[send_src[slot]]
-
-    arrived[slot_total] = jnp.zeros_like(arrived[slot_total])
-    first_ref[...] = jnp.zeros_like(first_ref)
-    second_ref[...] = jnp.zeros_like(second_ref)
-    bias_ref[...] = jnp.zeros_like(bias_ref)
-    arrived[pl.ds(me * CAP, CAP)] = leaving[pl.ds(me * CAP, CAP)]
+        leaving_t[slot] = targets[send_src[slot]]
+        leaving_f[slot] = frames[send_src[slot]]
+
+    own_slots = pl.ds(me * CAP, CAP)
+    arrived_t[slot_total] = jnp.zeros_like(arrived_t[slot_total])
+    arrived_f[slot_total] = jnp.zeros_like(arrived_f[slot_total])
+    arrived_t[own_slots] = leaving_t[own_slots]
+    arrived_f[own_slots] = leaving_f[own_slots]
 
     beside = has_right.astype(jnp.int32) + has_left.astype(jnp.int32)
     pl.semaphore_wait(barrier, owners - 1 + beside)
@@ -123,48 +129,86 @@
 
     @pl.loop(1, owners)
     def _(step):
-        route(leaving, arrived, send_a, recv_a, peer(step), me).start()
-
-    @pl.loop(1, owners)
-    def _(step):
-        other = peer(owners - step)
-        route(leaving, arrived, send_a, recv_a, other, other).wait_recv()
-
-    def relay(image, part_at, send_sem, to):
-        span = held.at[image, pl.ds(part_at * batch, batch)]
+        route(leaving_t, arrived_t, send_t, recv_t, peer(step), me).start()
+
+    @pl.loop(1, owners)
+    def _(step):
+        route(leaving_f, arrived_f, send_f, recv_f, peer(step), me).start()
+
+    first_ref[...] = jnp.zeros_like(first_ref)
+    second_ref[...] = jnp.zeros_like(second_ref)
+    bias_ref[...] = jnp.zeros_like(bias_ref)
+    cell = lax.broadcasted_iota(jnp.int32, (64, FRAME), 0)
+    place = lax.broadcasted_iota(jnp.int32, (64, FRAME), 1)
+    for shift in range(9):
+        wanted = (cell // 8 + shift // 3) * 10 + cell % 8 + shift % 3
+        pick[shift * 64 : (shift + 1) * 64, :] = jnp.where(wanted == place, 1.0, 0.0).astype(
+            jnp.bfloat16
+        )
+
+    def relay(held, image, first, size, unit, send_sem, to):
+        span = held.at[image, pl.ds(first, size)]
         return pltpu.make_async_remote_copy(
             src_ref=span,
             dst_ref=span,
-            send_sem=send_sem.at[image, part_at],
-            recv_sem=recv_z.at[image, part_at],
+            send_sem=send_sem.at[image, unit],
+            recv_sem=recv_z.at[image, unit],
             device_id=(me, to),
             device_id_type=MESH,
         )
 
-    def to_right(image, part_at):
-        return relay(image, part_at, send_right, z + 1)
-
-    def to_left(image, part_at):
-        return relay(image, part_at, send_left, z - 1)
+    def relay_t(image, send_sem, to):
+        return relay(held_t, image, 0, capacity, batches, send_sem, to)
+
+    def relay_f(image, part_at, send_sem, to):
+        return relay(held_f, image, part_at * batch, batch, part_at, send_sem, to)
+
+    def on_right(image, make):
+        @pl.when(has_right)
+        def _():
+            make(image, send_right, z + 1).start()
+
+    def on_left(image, make):
+        @pl.when(has_left)
+        def _():
+            make(image, send_left, z - 1).start()
+
+    def on_both(image, make):
+        @pl.when(has_right & (image <= z))
+        def _():
+            make(image, send_right, z + 1)
+
+        @pl.when(has_left & (image >= z))
+        def _():
+            make(image, send_left, z - 1)
+
+    def wait_all(source, target, send_sem, recv_sem):
+        @pl.loop(1, owners)
+        def _(step):
+            other = peer(owners - step)
+            route(source, target, send_sem, recv_sem, other, other).wait_recv()
+
+    wait_all(leaving_t, arrived_t, send_t, recv_t)
+
+    @pl.loop(0, capacity)
+    def _(tile):
+        held_t[z, tile] = arrived_t[take_src[tile]]
+
+    on_both(z, lambda *where: relay_t(*where).start())
+    wait_all(leaving_f, arrived_f, send_f, recv_f)
 
     @pl.loop(0, batches)
     def _(part_at):
         @pl.loop(0, batch)
         def _(within):
             tile = part_at * batch + within
-            held[z, tile] = arrived[take_src[tile]]
-
-        @pl.when(has_right)
-        def _():
-            to_right(z, part_at).start()
-
-        @pl.when(has_left)
-        def _():
-            to_left(z, part_at).start()
+            held_f[z, tile] = arrived_f[take_src[tile]]
+
+        on_both(z, lambda image, sem, to: relay_f(image, part_at, sem, to).start())
 
     def unfold(image, part_at):
         for within in range(batch):
-            frame = held[image, part_at * batch + within, 64:SLOT, :]
+            frame = held_f[image, part_at * batch + within]
             for shift in range(9):
                 patches[within * 64 : (within + 1) * 64, shift * channels : (shift + 1) * channels] = jnp.dot(
                     pick[shift * 64 : (shift + 1) * 64, :], frame, preferred_element_type=jnp.float32
@@ -176,13 +220,13 @@
     def preact_of(block):
         return (
             jnp.dot(patches[...], w_in[:, columns(block)], preferred_element_type=jnp.float32)
-            + b_in[pl.ds(block, 1), :]
+            + b_in[:, columns(block)]
         )
 
     def gradients(image, part_at):
         activation, slope = gelu_parts(preact_of(z))
         hidden = activation.astype(jnp.bfloat16)
-        target = held[image, pl.ds(part_at * batch, batch), 0:64, :].reshape(batch * 64, channels)
+        target = held_t[image, pl.ds(part_at * batch, batch)].reshape(batch * 64, channels)
         back = lax.dot_general(
             target,
             w_out[columns(z), :],
@@ -211,6 +255,8 @@
             batch, 64, channels
         )
 
+        gradients(z, part_at)
+
     @pl.loop(0, slot_total)
     def _(slot):
         going[slot] = result[back_src[slot]]
@@ -219,46 +265,53 @@
 
     @pl.loop(1, owners)
     def _(step):
-        route(going, returned, send_b, recv_b, peer(step), me).start()
-
-    @pl.loop(0, images * batches)
-    def _(index):
-        distance = index // batches
-        part_at = lax.rem(index, batches)
+        route(going, returned, send_o, recv_o, peer(step), me).start()
+
+    @pl.loop(1, images)
+    def _(distance):
         low = z - distance
         high = z + distance
-        arrives_low = (distance > 0) & (low >= 0)
-        arrives_high = (distance > 0) & (high < images)
+        arrives_low = low >= 0
+        arrives_high = high < images
 
         @pl.when(arrives_low)
         def _():
-            relay(low, part_at, send_right, z).wait_recv()
-
-            @pl.when(has_right)
+            relay_t(low, send_right, z).wait_recv()
+            on_right(low, relay_t)
+
+        @pl.when(arrives_high)
+        def _():
+            relay_t(high, send_left, z).wait_recv()
+            on_left(high, relay_t)
+
+        @pl.loop(0, batches)
+        def _(part_at):
+            def frames_of(image, send_sem, to):
+                return relay_f(image, part_at, send_sem, to)
+
+            @pl.when(arrives_low)
             def _():
-                to_right(low, part_at).start()
-
-        @pl.when(arrives_high)
-        def _():
-            relay(high, part_at, send_left, z).wait_recv()
-
-            @pl.when(has_left)
+                frames_of(low, send_right, z).wait_recv()
+                on_right(low, frames_of)
+
+            @pl.when(arrives_high)
             def _():
-                to_left(high, part_at).start()
-
-        @pl.loop(0, 2)
-        def _(side):
-            image = jnp.where(side == 0, low, high)
-
-            @pl.when((image >= 0) & (image < images) & ((distance > 0) | (side == 0)))
-            def _():
-                unfold(image, part_at)
-                gradients(image, part_at)
+                frames_of(high, send_left, z).wait_recv()
+                on_left(high, frames_of)
+
+            @pl.loop(0, 2)
+            def _(side):
+                image = jnp.where(side == 0, low, high)
+
+                @pl.when((image >= 0) & (image < images))
+                def _():
+                    unfold(image, part_at)
+                    gradients(image, part_at)
 
     @pl.loop(1, owners)
     def _(step):
         other = peer(owners - step)
-        route(going, returned, send_b, recv_b, other, other).wait_recv()
+        route(going, returned, send_o, recv_o, other, other).wait_recv()
 
     @pl.loop(0, tile_count)
     def _(tile):
@@ -267,29 +320,17 @@
     @pl.loop(1, owners)
     def _(step):
         other = peer(step)
-        route(leaving, arrived, send_a, recv_a, other, me).wait_send()
-        route(going, returned, send_b, recv_b, other, me).wait_send()
-
-    @pl.loop(0, images * batches)
-    def _(index):
-        image = index // batches
-        part_at = lax.rem(index, batches)
-
-        @pl.when(has_right & (image <= z))
-        def _():
-            to_right(image, part_at).wait_send()
-
-        @pl.when(has_left & (image >= z))
-        def _():
-            to_left(image, part_at).wait_send()
-
-
-def pick_matrix():
-    row = jnp.arange(9 * 64, dtype=jnp.int32)
-    shift = row // 64
-    cell = row % 64
-    wanted = (cell // 8 + shift // 3) * 10 + cell % 8 + shift % 3
-    return (wanted[:, None] == jnp.arange(FRAME, dtype=jnp.int32)[None, :]).astype(jnp.bfloat16)
+        route(leaving_t, arrived_t, send_t, recv_t, other, me).wait_send()
+        route(leaving_f, arrived_f, send_f, recv_f, other, me).wait_send()
+        route(going, returned, send_o, recv_o, other, me).wait_send()
+
+    @pl.loop(0, images)
+    def _(image):
+        on_both(image, lambda *where: relay_t(*where).wait_send())
+
+        @pl.loop(0, batches)
+        def _(part_at):
+            on_both(image, lambda here, sem, to: relay_f(here, part_at, sem, to).wait_send())
 
 
 def shards(heatmap, labels, w_in, w_out, b_in, cotangent):
@@ -303,7 +344,9 @@
     batch = max(b for b in range(1, 8) if capacity % b == 0)
     hidden_size = w_in.shape[2]
     part = hidden_size // images
-    every = lax.all_gather(labels[0], "expert", axis=0, tiled=False)
+    expert_ids = jnp.arange(owners, dtype=jnp.int32)
+    wanted = jnp.sum((labels[0][None, :] == expert_ids[:, None]).astype(jnp.int32), axis=1)
+    counts = lax.all_to_all(wanted, "expert", split_axis=0, concat_axis=0, tiled=True)
     bordered = extended(heatmap[0])
     bordered = jnp.pad(bordered, ((0, 0), (1, 7), (0, 0)))
     left_part = bordered[:, :columns].reshape(10, tile_count, 8, channels)
@@ -319,9 +362,7 @@
         .transpose(1, 0, 2, 3)
         .reshape(tile_count, 64, channels)
     )
-    tiles = jnp.concatenate([targets, framed], axis=1)
-    tiles = jnp.pad(tiles, ((0, 1), (0, SLOT - 164), (0, 0)))
-
+    frames = jnp.pad(framed, ((0, 0), (0, FRAME - 100), (0, 0)))
     labels_here = labels[0]
     tile_ids = jnp.arange(tile_count, dtype=jnp.int32)
     earlier = (labels_here[None, :] == labels_here[:, None]) & (
@@ -329,13 +370,9 @@
     )
     slot_index = labels_here * CAP + jnp.sum(earlier.astype(jnp.int32), axis=1)
     slot_ids = jnp.arange(slot_total, dtype=jnp.int32)
-    send_src = tile_count + jnp.sum(
-        jnp.where(
-            slot_index[None, :] == slot_ids[:, None], tile_ids[None, :] - tile_count, 0
-        ),
-        axis=1,
-    )
-    counts = jnp.sum((every == lax.axis_index("expert")).astype(jnp.int32), axis=1)
+    send_src = jnp.sum(
+        jnp.where(slot_index[None, :] == slot_ids[:, None], tile_ids[None, :], 0), axis=1
+    )
     live = (slot_ids % CAP) < jnp.broadcast_to(counts[:, None], (owners, CAP)).reshape(slot_total)
     position = jnp.sum(
         ((slot_ids[None, :] < slot_ids[:, None]) & live[None, :]).astype(jnp.int32), axis=1
@@ -367,21 +404,20 @@
         in_specs=[smem] * 4 + [vmem] * 5,
         out_specs=(vmem,) * 4,
         scratch_shapes=[
-            pltpu.VMEM((slot_total, SLOT, channels), bf16),
-            pltpu.VMEM((slot_total + 1, SLOT, channels), bf16),
-            pltpu.VMEM((images, capacity, SLOT, channels), bf16),
+            pltpu.VMEM((slot_total, 64, channels), bf16),
+            pltpu.VMEM((slot_total, FRAME, channels), bf16),
+            pltpu.VMEM((slot_total + 1, 64, channels), bf16),
+            pltpu.VMEM((slot_total + 1, FRAME, channels), bf16),
+            pltpu.VMEM((images, capacity, 64, channels), bf16),
+            pltpu.VMEM((images, capacity, FRAME, channels), bf16),
+            pltpu.VMEM((9 * 64, FRAME), bf16),
             pltpu.VMEM((batch * 64, 9 * channels), bf16),
             pltpu.VMEM((capacity, 64, channels), bf16),
             pltpu.VMEM((slot_total, 64, channels), bf16),
             pltpu.VMEM((slot_total, 64, channels), bf16),
-            dma((owners,)),
-            dma((owners,)),
-            dma((owners,)),
-            dma((owners,)),
-            dma((images, batches)),
-            dma((images, batches)),
-            dma((images, batches)),
-        ],
+        ]
+        + [dma((owners,))] * 6
+        + [dma((images, batches + 1))] * 3,
         compiler_params=pltpu.CompilerParams(
             collective_id=0, has_side_effects=True, vmem_limit_bytes=60 * 2**20
         ),
@@ -390,11 +426,11 @@
         take_src,
         back_src,
         slot_index,
-        tiles,
-        pick_matrix(),
+        targets,
+        frames,
         w_in[0],
         w_out[0],
-        b_in[0].reshape(images, part),
+        b_in,
     )
     output = (
         out.reshape(tile_count, 8, 8, channels)

time: 118 us -> 108 us (0.915)
  blocking collectives: 10.1 us -> 0 us
  starting transfers between devices: 6.42 us -> 10.7 us
  Pallas kernels: 83.7 us -> 80.3 us
  other arithmetic: 8.6 us -> 6.86 us
    all_gather x1 -> x0, blocking collectives: 10.1 us -> none  [shards(): every = lax.all_gather(labels[0], 'expert', axis=0, tiled=False)]
    all_to_all x0 -> x1, starting transfers between devices: none -> 5.22 us  [shards(): lax.all_to_all(wanted, 'expert', split_axis=0, concat_axis=0, tiled=True)]
    pallas_call x1, Pallas kernels: 83.7 us -> 80.3 us  [shards(): pl.pallas_call(functools.partial(kernel, owners, images, batch), out_shap...]
    unnamed x1 -> x0, other arithmetic: 1.35 us -> none
    unnamed x11 -> x10, local copies, waits for them, and re-layouts: 4.89 us -> 4.38 us
  transfers between devices with their start and end apart: 2 -> 3, of which waited for: 0 -> 0; matrix products, arithmetic and copies ran while one was open for 7% -> 6% of each run, Pallas kernels for 0% -> 0%
where the time goes in v3:
time: 108 us
  Pallas kernels  80.3 us (74%)
  starting transfers between devices  10.7 us (10%)
  local copies, waits for them, and re-layouts  9.32 us (9%)
  other arithmetic  6.86 us (6%)
    pallas_call x1, Pallas kernels, shards(): pl.pallas_call(functools.partial(kernel, owners, images, batch), out_shap...  80.3 us
    all_to_all x1, starting transfers between devices, shards(): lax.all_to_all(wanted, 'expert', split_axis=0, concat_axis=0, tiled=True)  5.22 us
    unnamed x10, local copies, waits for them, and re-layouts  4.38 us
    ppermute x1, starting transfers between devices, extended(): lax.ppermute(cells[-1:], 'expert', [(i, i + 1) for i in range(ends)])  3.53 us
  transfers between devices with their start and end apart: 3, of which 0 were waited for; matrix products, arithmetic and copies ran while one was open for 6% of the time, Pallas kernels for 0%

profile of v3, /device:TPU:1, one launch (start us, length us, event | category | flops | bytes accessed | tf_op | source)
XLA Modules:
  0.0 107.9 jit_solution(3190478605548177984)
XLA Ops:
  0.6 0.8 convert_reduce_fusion.1
  1.5 0.7 copy.35
  2.1 5.2 %all-to-all-start = ((s32[8,1,1]{2,1,0:T(1,128)}), s32[8,1,1]{2,1,0:T(1,128)S(1)}, u32[]{:S(2)}, u32[]{:S(2)}) async-start(s32[8,1,1]{2,1,0:T(1,128)} %copy.35), calls=%async_computation | async-start | bytes 8192 | tf_op jit(solution)/shard_map/all_to_all | solution.py:349
  7.4 0.8 slice_bitcast_fusion.3
  8.1 3.5 %collective-permute-start = (bf16[1,56,256]{2,1,0:T(8,128)(2,1)S(1)}, bf16[1,56,256]{2,1,0:T(8,128)(2,1)S(1)}, u32[]{:S(2)}, u32[]{:S(2)}) collective-permute-start(bf16[1,56,256]{2,1,0:T(8,128)(2,1)S(1)} %get-tuple-element.34), channel_id=1, source_target_pairs={{0,4},{4,8},{8,12},{12,16},{16,20},{20,24},{24,28},{1,5},{5,9},{9,... | collective-permute-start | bytes 86024 | tf_op jit(solution)/shard_map/ppermute | solution.py:20
  11.7 1.9 %collective-permute-start.1 = (bf16[1,56,256]{2,1,0:T(8,128)(2,1)S(1)}, bf16[1,56,256]{2,1,0:T(8,128)(2,1)S(1)}, u32[]{:S(2)}, u32[]{:S(2)}) collective-permute-start(bf16[1,56,256]{2,1,0:T(8,128)(2,1)S(1)} %get-tuple-element.35), channel_id=1, source_target_pairs={{4,0},{8,4},{12,8},{16,12},{20,16},{24,20},{28,24},{5,1},{9,5},{13... | collective-permute-start | bytes 86024 | tf_op jit(solution)/shard_map/ppermute | solution.py:22
  13.6 0.9 convert_reduce_fusion.2
  14.5 1.2 %multiply_add_fusion.mine_src = s32[7]{0:T(128)} fusion(s32[7]{0:T(128)S(1)} %convert_reduce_fusion.2, s32[1,7]{1,0:T(1,128)} %param.7), kind=kLoop, calls=%fused_computation.32 | loop fusion | flops 14 | bytes 84 | tf_op jit(solution)/shard_map/add | solution.py:371
  15.7 0.7 fusion.10
  16.4 0.6 select_reduce_fusion.1.send_src
  17.0 0.7 copy_bitcast_fusion.1.targets
  17.7 0.2 reduce
  18.1 0.1 convert_reduce_fusion
  18.2 0.5 broadcast_minimum_fusion.back_src
  18.8 0.1 select_reduce_fusion
  18.9 0.5 broadcast_add_fusion.take_src
  19.4 1.0 fusion.5
  20.6 0.1 pad_maximum_fusion
  20.8 0.8 pad.9.frames
  21.6 80.3 %shard_map.93 = (bf16[7,64,256]{2,1,0:T(8,128)(2,1)}, f32[256,2304]{1,0:T(8,128)}, f32[256,256]{1,0:T(8,128)}, f32[1,256]{1,0:T(1,128)}) custom-call(s32[16]{0:T(128)} %select_reduce_fusion.1.send_src, s32[10]{0:T(128)} %broadcast_add_fusion.take_src, s32[16]{0:T(128)} %broadcast_minimum_fusion.back_src, s32[7]{0:T(128)} %multiply_add_fusion.mine_src, ...), custom_call_target="tpu_custom_call" | custom-call | tf_op jit(solution)/shard_map/pallas_call | solution.py:396
  101.9 1.6 %copy_bitcast_fusion = bf16[1,8,56,256]{3,2,1,0:T(8,128)(2,1)} fusion(bf16[7,64,256]{2,1,0:T(8,128)(2,1)} %get-tuple-element.8), kind=kLoop, calls=%fused_computation.11 | loop fusion | bytes 458752 | tf_op jit(solution)/shard_map/reshape | solution.py:438
  103.6 3.1 %copy.41 = f32[1,2304,256]{2,1,0:T(8,128)} copy(f32[1,2304,256]{1,2,0:T(8,128)} %bitcast.42) | data formatting | bytes 4718592
  106.7 0.7 copy.47
  107.4 0.6 copy.48
  (18 shorter events, 0.4 us)
Async XLA Ops:
  0.6 16.4 %copy-start = (bf16[1,8,56,256]{3,2,1,0:T(8,128)(2,1)S(1)}, bf16[1,8,56,256]{3,2,1,0:T(8,128)(2,1)}, u32[]{:S(2)}) copy-start(bf16[1,8,56,256]{3,2,1,0:T(8,128)(2,1)} %param.11) | copy-start | bytes 688132
  2.1 15.6 %all-to-all-start = ((s32[8,1,1]{2,1,0:T(1,128)}), s32[8,1,1]{2,1,0:T(1,128)S(1)}, u32[]{:S(2)}, u32[]{:S(2)}) async-start(s32[8,1,1]{2,1,0:T(1,128)} %copy.35), calls=%async_computation | async-start | bytes 8192 | tf_op jit(solution)/shard_map/all_to_all | solution.py:349
  8.1 11.3 %collective-permute-start = (bf16[1,56,256]{2,1,0:T(8,128)(2,1)S(1)}, bf16[1,56,256]{2,1,0:T(8,128)(2,1)S(1)}, u32[]{:S(2)}, u32[]{:S(2)}) collective-permute-start(bf16[1,56,256]{2,1,0:T(8,128)(2,1)S(1)} %get-tuple-element.34), channel_id=1, source_target_pairs={{0,4},{4,8},{8,12},{12,16},{16,20},{20,24},{24,28},{1,5},{5,9},{9,... | collective-permute-start | bytes 86024 | tf_op jit(solution)/shard_map/ppermute | solution.py:20
  11.7 7.7 %collective-permute-start.1 = (bf16[1,56,256]{2,1,0:T(8,128)(2,1)S(1)}, bf16[1,56,256]{2,1,0:T(8,128)(2,1)S(1)}, u32[]{:S(2)}, u32[]{:S(2)}) collective-permute-start(bf16[1,56,256]{2,1,0:T(8,128)(2,1)S(1)} %get-tuple-element.35), channel_id=1, source_target_pairs={{4,0},{8,4},{12,8},{16,12},{20,16},{24,20},{28,24},{5,1},{9,5},{13... | collective-permute-start | bytes 86024 | tf_op jit(solution)/shard_map/ppermute | solution.py:22
  103.6 3.1 %copy-start.1 = (f32[256,256]{1,0:T(8,128)S(1)}, f32[256,256]{1,0:T(8,128)}, u32[]{:S(2)}) copy-start(f32[256,256]{1,0:T(8,128)} %get-tuple-element.10) | copy-start | bytes 786436
  103.6 3.8 %copy-start.2 = (f32[1,256]{1,0:T(1,128)S(1)}, f32[1,256]{1,0:T(1,128)}, u32[]{:S(2)}) copy-start(f32[1,256]{1,0:T(1,128)} %get-tuple-element.43) | copy-start | bytes 3076

commit v4 on v3

--- a/solution.py
+++ b/solution.py
@@ -238,6 +238,22 @@
         bias_ref[...] += jnp.sum(hidden_grad.astype(jnp.float32), axis=0, keepdims=True)
         first_ref[...] += contract_rows(hidden_grad, patches[...])
 
+    def pass_targets(distance):
+        low = z - distance
+        high = z + distance
+
+        @pl.when(low >= 0)
+        def _():
+            relay_t(low, send_right, z).wait_recv()
+            on_right(low, relay_t)
+
+        @pl.when(high < images)
+        def _():
+            relay_t(high, send_left, z).wait_recv()
+            on_left(high, relay_t)
+
+    pass_targets(1)
+
     @pl.loop(0, batches)
     def _(part_at):
         unfold(z, part_at)
@@ -274,15 +290,9 @@
         arrives_low = low >= 0
         arrives_high = high < images
 
-        @pl.when(arrives_low)
-        def _():
-            relay_t(low, send_right, z).wait_recv()
-            on_right(low, relay_t)
-
-        @pl.when(arrives_high)
-        def _():
-            relay_t(high, send_left, z).wait_recv()
-            on_left(high, relay_t)
+        @pl.when(distance > 1)
+        def _():
+            pass_targets(distance)
 
         @pl.loop(0, batches)
         def _(part_at):

time: 108 us -> 108 us (level)
  no operation moved by 1% of the time
where the time goes in v4:
time: 108 us
  Pallas kernels  80.3 us (74%)
  starting transfers between devices  10.7 us (10%)
  local copies, waits for them, and re-layouts  9.32 us (9%)
  other arithmetic  6.86 us (6%)
    pallas_call x1, Pallas kernels, shards(): pl.pallas_call(functools.partial(kernel, owners, images, batch), out_shap...  80.3 us
    all_to_all x1, starting transfers between devices, shards(): lax.all_to_all(wanted, 'expert', split_axis=0, concat_axis=0, tiled=True)  5.22 us
    unnamed x10, local copies, waits for them, and re-layouts  4.38 us
    ppermute x1, starting transfers between devices, extended(): lax.ppermute(cells[-1:], 'expert', [(i, i + 1) for i in range(ends)])  3.53 us
  transfers between devices with their start and end apart: 3, of which 0 were waited for; matrix products, arithmetic and copies ran while one was open for 6% of the time, Pallas kernels for 0%

profile of v4, /device:TPU:1, one launch (start us, length us, event | category | flops | bytes accessed | tf_op | source)
XLA Modules:
  0.0 107.9 jit_solution(16858874791677380136)
XLA Ops:
  0.6 0.8 convert_reduce_fusion.1
  1.5 0.7 copy.35
  2.1 5.2 %all-to-all-start = ((s32[8,1,1]{2,1,0:T(1,128)}), s32[8,1,1]{2,1,0:T(1,128)S(1)}, u32[]{:S(2)}, u32[]{:S(2)}) async-start(s32[8,1,1]{2,1,0:T(1,128)} %copy.35), calls=%async_computation | async-start | bytes 8192 | tf_op jit(solution)/shard_map/all_to_all | solution.py:359
  7.4 0.8 slice_bitcast_fusion.3
  8.1 3.5 %collective-permute-start = (bf16[1,56,256]{2,1,0:T(8,128)(2,1)S(1)}, bf16[1,56,256]{2,1,0:T(8,128)(2,1)S(1)}, u32[]{:S(2)}, u32[]{:S(2)}) collective-permute-start(bf16[1,56,256]{2,1,0:T(8,128)(2,1)S(1)} %get-tuple-element.34), channel_id=1, source_target_pairs={{0,4},{4,8},{8,12},{12,16},{16,20},{20,24},{24,28},{1,5},{5,9},{9,... | collective-permute-start | bytes 86024 | tf_op jit(solution)/shard_map/ppermute | solution.py:20
  11.7 1.9 %collective-permute-start.1 = (bf16[1,56,256]{2,1,0:T(8,128)(2,1)S(1)}, bf16[1,56,256]{2,1,0:T(8,128)(2,1)S(1)}, u32[]{:S(2)}, u32[]{:S(2)}) collective-permute-start(bf16[1,56,256]{2,1,0:T(8,128)(2,1)S(1)} %get-tuple-element.35), channel_id=1, source_target_pairs={{4,0},{8,4},{12,8},{16,12},{20,16},{24,20},{28,24},{5,1},{9,5},{13... | collective-permute-start | bytes 86024 | tf_op jit(solution)/shard_map/ppermute | solution.py:22
  13.6 0.9 convert_reduce_fusion.2
  14.5 1.2 %multiply_add_fusion.mine_src = s32[7]{0:T(128)} fusion(s32[7]{0:T(128)S(1)} %convert_reduce_fusion.2, s32[1,7]{1,0:T(1,128)} %param.7), kind=kLoop, calls=%fused_computation.32 | loop fusion | flops 14 | bytes 84 | tf_op jit(solution)/shard_map/add | solution.py:381
  15.7 0.7 fusion.10
  16.4 0.6 select_reduce_fusion.1.send_src
  17.0 0.7 copy_bitcast_fusion.1.targets
  17.7 0.2 reduce
  18.1 0.1 convert_reduce_fusion
  18.2 0.5 broadcast_minimum_fusion.back_src
  18.8 0.1 select_reduce_fusion
  18.9 0.5 broadcast_add_fusion.take_src
  19.4 1.0 fusion.5
  20.6 0.1 pad_maximum_fusion
  20.8 0.8 pad.9.frames
  21.6 80.3 %shard_map.93 = (bf16[7,64,256]{2,1,0:T(8,128)(2,1)}, f32[256,2304]{1,0:T(8,128)}, f32[256,256]{1,0:T(8,128)}, f32[1,256]{1,0:T(1,128)}) custom-call(s32[16]{0:T(128)} %select_reduce_fusion.1.send_src, s32[10]{0:T(128)} %broadcast_add_fusion.take_src, s32[16]{0:T(128)} %broadcast_minimum_fusion.back_src, s32[7]{0:T(128)} %multiply_add_fusion.mine_src, ...), custom_call_target="tpu_custom_call" | custom-call | tf_op jit(solution)/shard_map/pallas_call | solution.py:406
  101.9 1.6 %copy_bitcast_fusion = bf16[1,8,56,256]{3,2,1,0:T(8,128)(2,1)} fusion(bf16[7,64,256]{2,1,0:T(8,128)(2,1)} %get-tuple-element.8), kind=kLoop, calls=%fused_computation.11 | loop fusion | bytes 458752 | tf_op jit(solution)/shard_map/reshape | solution.py:448
  103.6 3.1 %copy.41 = f32[1,2304,256]{2,1,0:T(8,128)} copy(f32[1,2304,256]{1,2,0:T(8,128)} %bitcast.42) | data formatting | bytes 4718592
  106.7 0.7 copy.47
  107.4 0.6 copy.48
  (18 shorter events, 0.4 us)
Async XLA Ops:
  0.6 16.4 %copy-start = (bf16[1,8,56,256]{3,2,1,0:T(8,128)(2,1)S(1)}, bf16[1,8,56,256]{3,2,1,0:T(8,128)(2,1)}, u32[]{:S(2)}) copy-start(bf16[1,8,56,256]{3,2,1,0:T(8,128)(2,1)} %param.11) | copy-start | bytes 688132
  2.1 15.6 %all-to-all-start = ((s32[8,1,1]{2,1,0:T(1,128)}), s32[8,1,1]{2,1,0:T(1,128)S(1)}, u32[]{:S(2)}, u32[]{:S(2)}) async-start(s32[8,1,1]{2,1,0:T(1,128)} %copy.35), calls=%async_computation | async-start | bytes 8192 | tf_op jit(solution)/shard_map/all_to_all | solution.py:359
  8.1 11.3 %collective-permute-start = (bf16[1,56,256]{2,1,0:T(8,128)(2,1)S(1)}, bf16[1,56,256]{2,1,0:T(8,128)(2,1)S(1)}, u32[]{:S(2)}, u32[]{:S(2)}) collective-permute-start(bf16[1,56,256]{2,1,0:T(8,128)(2,1)S(1)} %get-tuple-element.34), channel_id=1, source_target_pairs={{0,4},{4,8},{8,12},{12,16},{16,20},{20,24},{24,28},{1,5},{5,9},{9,... | collective-permute-start | bytes 86024 | tf_op jit(solution)/shard_map/ppermute | solution.py:20
  11.7 7.7 %collective-permute-start.1 = (bf16[1,56,256]{2,1,0:T(8,128)(2,1)S(1)}, bf16[1,56,256]{2,1,0:T(8,128)(2,1)S(1)}, u32[]{:S(2)}, u32[]{:S(2)}) collective-permute-start(bf16[1,56,256]{2,1,0:T(8,128)(2,1)S(1)} %get-tuple-element.35), channel_id=1, source_target_pairs={{4,0},{8,4},{12,8},{16,12},{20,16},{24,20},{28,24},{5,1},{9,5},{13... | collective-permute-start | bytes 86024 | tf_op jit(solution)/shard_map/ppermute | solution.py:22
  103.6 3.1 %copy-start.1 = (f32[256,256]{1,0:T(8,128)S(1)}, f32[256,256]{1,0:T(8,128)}, u32[]{:S(2)}) copy-start(f32[256,256]{1,0:T(8,128)} %get-tuple-element.10) | copy-start | bytes 786436
  103.6 3.8 %copy-start.2 = (f32[1,256]{1,0:T(1,128)S(1)}, f32[1,256]{1,0:T(1,128)}, u32[]{:S(2)}) copy-start(f32[1,256]{1,0:T(1,128)} %get-tuple-element.43) | copy-start | bytes 3076
